TPU v7x, 32 devices: a whole 2x2x4 slice. The times are simulated.
32 devices in a mesh: pipe: 2 (over x), dp: 16 (over z, y, core).
Axes of the slice: x: 2, y: 2, z: 4, core: 2. Of those that a mesh axis runs over, the one named last changes fastest.
Arguments:
- inputs: bfloat16 [64, 256, 768], P('dp'), may hold values from -6 to 6
- cotangent: bfloat16 [64, 256, 768], P('dp'), may hold values from -6 to 6
- lengths: int32 [64], P('dp'), may hold values from 128 to 256, as said below
- norm1_gain: float32 [2, 768], P('pipe'), may hold values from 0.5 to 1.5
- norm1_bias: float32 [2, 768], P('pipe'), may hold values from -1 to 1
- qkv_weight: bfloat16 [2, 768, 2304], P('pipe'), may hold values from -0.21875 to 0.21875
- qkv_bias: float32 [2, 2304], P('pipe'), may hold values from -1 to 1
- dense_weight: bfloat16 [2, 768, 768], P('pipe'), may hold values from -1.25 to 1.25
- dense_bias: float32 [2, 768], P('pipe'), may hold values from -1 to 1
- norm2_gain: float32 [2, 768], P('pipe'), may hold values from 0.5 to 1.5
- norm2_bias: float32 [2, 768], P('pipe'), may hold values from -1 to 1
- fc_in_weight: bfloat16 [2, 768, 3072], P('pipe'), may hold values from -0.21875 to 0.21875
- fc_in_bias: float32 [2, 3072], P('pipe'), may hold values from -1 to 1
- fc_out_weight: bfloat16 [2, 3072, 768], P('pipe'), may hold values from -0.109375 to 0.109375
- fc_out_bias: float32 [2, 768], P('pipe'), may hold values from -1 to 1
Outputs:
- layer_outputs: bfloat16 [2, 64, 256, 768], P('pipe', 'dp')
- input_grads: bfloat16 [2, 64, 256, 768], P('pipe', 'dp')
- grad_norm1_gain: float32 [2, 768], P('pipe')
- grad_norm1_bias: float32 [2, 768], P('pipe')
- grad_qkv_weight: float32 [2, 768, 2304], P('pipe')
- grad_qkv_bias: float32 [2, 2304], P('pipe')
- grad_dense_weight: float32 [2, 768, 768], P('pipe')
- grad_dense_bias: float32 [2, 768], P('pipe')
- grad_norm2_gain: float32 [2, 768], P('pipe')
- grad_norm2_bias: float32 [2, 768], P('pipe')
- grad_fc_in_weight: float32 [2, 768, 3072], P('pipe')
- grad_fc_in_bias: float32 [2, 3072], P('pipe')
- grad_fc_out_weight: float32 [2, 3072, 768], P('pipe')
- grad_fc_out_bias: float32 [2, 768], P('pipe')
- example_norms: float32 [64], P('dp')
Inputs may be any that keep to these rules, and one draw needn't show every extreme that they name: `lengths`: each sequence has between 128 and 256 tokens; in every draw some sequence has exactly 256.
All inputs are finite; a program needn't handle non-finite values.
Results may differ from a plain program's by a relative error of at most 0.017.
Values may be sent and summed in bfloat16 or wider, within the bound.
A program may use at most 256 MiB of HBM per device.

v0:
```python
import jax
import jax.numpy as jnp
from jax import lax
from jax.sharding import PartitionSpec as P

D = 768
HEADS = 12
HEAD = 64
ROT = 16


EPSILON = 1e-05
NEG_FILL = -1e30
INV_ROOT_TWO = 0.7071067811865476
INV_ROOT_TWO_PI = 0.3989422804014327


def passed_along(array, axis, by):
    size = lax.axis_size(axis)
    pairs = [(i, i + by) for i in range(size) if 0 <= i + by < size]
    return lax.ppermute(array, axis, pairs)


def product(left, right):
    return jnp.dot(left, right, preferred_element_type=jnp.float32)


def product_tn(left, right):
    return lax.dot_general(
        left, right, (((0,), (0,)), ((), ())), preferred_element_type=jnp.float32
    )


def product_nt(left, right):
    return lax.dot_general(
        left, right, (((1,), (1,)), ((), ())), preferred_element_type=jnp.float32
    )


def flatten_all(leaves):
    return jnp.concatenate([leaf.reshape(-1) for leaf in leaves])


def split_back(flat, like):
    pieces = []
    offset = 0
    for leaf in like:
        count = leaf.size
        pieces.append(flat[offset : offset + count].reshape(leaf.shape))
        offset = offset + count
    return tuple(pieces)


def norm_parts(values, gain, shift):
    center = values - jnp.mean(values, axis=-1, keepdims=True)
    spread = jnp.mean(center * center, axis=-1, keepdims=True)
    inverse = lax.rsqrt(spread + EPSILON)
    unit = center * inverse
    return (unit * gain + shift, unit, inverse)


def norm_back(grad, unit, inverse, gain):
    scaled = grad * gain
    back = inverse * (
        scaled
        - jnp.mean(scaled, axis=-1, keepdims=True)
        - unit * jnp.mean(scaled * unit, axis=-1, keepdims=True)
    )
    return (back, jnp.sum(grad * unit, axis=0), jnp.sum(grad, axis=0))


def rotary_tables(seq_len):
    half = ROT // 2
    freq = jnp.power(10000.0, -(2.0 * jnp.arange(half, dtype=jnp.float32)) / ROT)
    angle = jnp.arange(seq_len, dtype=jnp.float32)[:, None] * freq[None, :]
    return (jnp.cos(angle)[:, None, :], jnp.sin(angle)[:, None, :])


def rotate(values, cosine, sine):
    half = ROT // 2
    first = values[..., :half]
    second = values[..., half:ROT]
    return jnp.concatenate(
        [first * cosine - second * sine, second * cosine + first * sine, values[..., ROT:]], axis=-1
    )


def allowed_keys(seq_len, length):
    positions = jnp.arange(seq_len)
    return (positions[None, :] <= positions[:, None]) & (positions[None, :] < length)


def forward(layer_in, weights, length, tables):
    gain1, shift1, w_qkv, b_qkv, w_dense, b_dense, gain2, shift2, w_in, b_in, w_out, b_out = weights
    cosine, sine = tables
    inp = layer_in.astype(jnp.float32)
    seq_len = inp.shape[0]
    normed1_f, unit1, inverse1 = norm_parts(inp, gain1, shift1)
    normed1 = normed1_f.astype(jnp.bfloat16)
    mixed = (product(normed1, w_qkv) + b_qkv).reshape(seq_len, 3, HEADS, HEAD)
    query = rotate(mixed[:, 0], cosine, sine).astype(jnp.bfloat16)
    key_rot = rotate(mixed[:, 1], cosine, sine).astype(jnp.bfloat16)
    value = mixed[:, 2].astype(jnp.bfloat16)
    scores = jnp.einsum(
        "qhd,khd->hqk", query, key_rot, preferred_element_type=jnp.float32
    ) * HEAD ** (-0.5)
    masked = jnp.where(allowed_keys(seq_len, length)[None], scores, NEG_FILL)
    top = jnp.max(masked, axis=-1, keepdims=True)
    expo = jnp.exp(masked - top)
    totals = jnp.sum(expo, axis=-1, keepdims=True)
    probs = (expo / totals).astype(jnp.bfloat16)
    log_total = top + jnp.log(totals)
    context = (
        jnp.einsum("hqk,khd->qhd", probs, value, preferred_element_type=jnp.float32)
        .reshape(seq_len, D)
        .astype(jnp.bfloat16)
    )
    attended = product(context, w_dense) + b_dense
    normed2_f, unit2, inverse2 = norm_parts(inp, gain2, shift2)
    normed2 = normed2_f.astype(jnp.bfloat16)
    hidden = product(normed2, w_in) + b_in
    activated = jax.nn.gelu(hidden, approximate=False).astype(jnp.bfloat16)
    result = inp + attended + product(activated, w_out) + b_out
    kept = (
        unit1,
        inverse1,
        normed1,
        query,
        key_rot,
        value,
        log_total,
        context,
        unit2,
        inverse2,
        normed2,
        hidden,
        activated,
    )
    return (result, kept)


def backward_inputs(grad_out, kept, weights, length, tables):
    gain1, shift1, w_qkv, b_qkv, w_dense, b_dense, gain2, shift2, w_in, b_in, w_out, b_out = weights
    (
        unit1,
        inverse1,
        normed1,
        query,
        key_rot,
        value,
        log_total,
        context,
        unit2,
        inverse2,
        normed2,
        hidden,
        activated,
    ) = kept
    cosine, sine = tables
    seq_len = grad_out.shape[0]
    grad_f = grad_out.astype(jnp.float32)
    grad_act = product_nt(grad_out, w_out)
    slope = (
        0.5 * (1.0 + lax.erf(hidden * INV_ROOT_TWO))
        + hidden * jnp.exp(-0.5 * hidden * hidden) * INV_ROOT_TWO_PI
    )
    grad_hidden = (grad_act * slope).astype(jnp.bfloat16)
    grad_normed2 = product_nt(grad_hidden, w_in)
    grad_context = product_nt(grad_out, w_dense).astype(jnp.bfloat16).reshape(seq_len, HEADS, HEAD)
    scores = jnp.einsum(
        "qhd,khd->hqk", query, key_rot, preferred_element_type=jnp.float32
    ) * HEAD ** (-0.5)
    probs = jnp.where(allowed_keys(seq_len, length)[None], jnp.exp(scores - log_total), 0.0)
    grad_value = jnp.einsum(
        "hqk,qhd->khd", probs.astype(jnp.bfloat16), grad_context, preferred_element_type=jnp.float32
    )
    grad_probs = jnp.einsum("qhd,khd->hqk", grad_context, value, preferred_element_type=jnp.float32)
    grad_scores = (
        probs * (grad_probs - jnp.sum(grad_probs * probs, axis=-1, keepdims=True))
    ).astype(jnp.bfloat16)
    grad_query = jnp.einsum(
        "hqk,khd->qhd", grad_scores, key_rot, preferred_element_type=jnp.float32
    ) * HEAD ** (-0.5)
    grad_key = jnp.einsum(
        "hqk,qhd->khd", grad_scores, query, preferred_element_type=jnp.float32
    ) * HEAD ** (-0.5)
    grad_mixed = jnp.stack(
        [rotate(grad_query, cosine, -sine), rotate(grad_key, cosine, -sine), grad_value], axis=1
    )
    grad_mixed = grad_mixed.reshape(seq_len, 3 * D).astype(jnp.bfloat16)
    grad_normed1 = product_nt(grad_mixed, w_qkv)
    back1, grad_gain1, grad_shift1 = norm_back(grad_normed1, unit1, inverse1, gain1)
    back2, grad_gain2, grad_shift2 = norm_back(grad_normed2, unit2, inverse2, gain2)
    grad_in = grad_f + back1 + back2
    operands = (normed1, grad_mixed, context, grad_out, normed2, grad_hidden, activated)
    norm_grads = (grad_gain1, grad_shift1, grad_gain2, grad_shift2)
    return (grad_in, operands, norm_grads)


def output_side(operands):
    normed1, grad_mixed, context, grad_out, normed2, grad_hidden, activated = operands
    grad_b = jnp.sum(grad_out.astype(jnp.float32), axis=0)
    return (product_tn(context, grad_out), grad_b, product_tn(activated, grad_out), grad_b)


def input_side(operands):
    normed1, grad_mixed, context, grad_out, normed2, grad_hidden, activated = operands
    return (
        product_tn(normed1, grad_mixed),
        jnp.sum(grad_mixed.astype(jnp.float32), axis=0),
        product_tn(normed2, grad_hidden),
        jnp.sum(grad_hidden.astype(jnp.float32), axis=0),
    )


def arrange(norm_grads, outer, inner):
    return (
        norm_grads[0],
        norm_grads[1],
        inner[0],
        inner[1],
        outer[0],
        outer[1],
        norm_grads[2],
        norm_grads[3],
        inner[2],
        inner[3],
        outer[2],
        outer[3],
    )


def squares(leaves):
    total = jnp.float32(0.0)
    for leaf in leaves:
        total = total + jnp.sum(leaf * leaf)
    return total


def on_device(
    inputs,
    cotangent,
    lengths,
    norm1_gain,
    norm1_bias,
    qkv_weight,
    qkv_bias,
    dense_weight,
    dense_bias,
    norm2_gain,
    norm2_bias,
    fc_in_weight,
    fc_in_bias,
    fc_out_weight,
    fc_out_bias,
):
    weights = tuple(
        (
            w[0]
            for w in (
                norm1_gain,
                norm1_bias,
                qkv_weight,
                qkv_bias,
                dense_weight,
                dense_bias,
                norm2_gain,
                norm2_bias,
                fc_in_weight,
                fc_in_bias,
                fc_out_weight,
                fc_out_bias,
            )
        )
    )
    sections = lax.axis_size("pipe")
    section = lax.axis_index("pipe")
    micro = inputs.shape[0]
    seq_len = inputs.shape[1]
    ticks = micro + sections - 1
    tables = rotary_tables(seq_len)
    first_section = section == 0
    last_section = section == sections - 1
    positions = jnp.arange(seq_len)

    def forward_tick(received, tick):
        index = tick - section
        clipped = jnp.clip(index, 0, micro - 1)
        own = lax.dynamic_index_in_dim(inputs, jnp.clip(tick, 0, micro - 1), 0, keepdims=False)
        layer_in = jnp.where(first_section, own, received)
        length = lax.dynamic_index_in_dim(lengths, clipped, 0, keepdims=False)
        result, kept = forward(layer_in, weights, length, tables)
        sent = result.astype(jnp.bfloat16)
        passed = passed_along(sent, "pipe", 1)
        return (passed, (sent, layer_in))

    start = jnp.zeros((seq_len, D), jnp.bfloat16)
    unused, (sent_all, saved_all) = lax.scan(forward_tick, start, jnp.arange(ticks))
    outputs_local = lax.dynamic_slice_in_dim(sent_all, section, micro, 0)

    def backward_tick(carry, tick):
        received, totals = carry
        index = tick - (sections - 1 - section)
        valid = (index >= 0) & (index < micro)
        clipped = jnp.clip(index, 0, micro - 1)
        length = lax.dynamic_index_in_dim(lengths, clipped, 0, keepdims=False)
        own_cot = lax.dynamic_index_in_dim(cotangent, clipped, 0, keepdims=False)
        masked_cot = jnp.where((positions < length)[:, None], own_cot, jnp.zeros_like(own_cot))
        grad_out = jnp.where(last_section, masked_cot, received)
        forward_slot = clipped + section
        layer_in = lax.dynamic_index_in_dim(saved_all, forward_slot, 0, keepdims=False)
        unused_out, kept = forward(layer_in, weights, length, tables)
        grad_in, operands, norm_grads = backward_inputs(grad_out, kept, weights, length, tables)
        norm_grads = tuple((jnp.where(valid, leaf, jnp.zeros_like(leaf)) for leaf in norm_grads))
        sent = grad_in.astype(jnp.bfloat16)
        passed = passed_along(sent, "pipe", -1)
        grads = arrange(norm_grads, output_side(operands), input_side(operands))
        grads = tuple((jnp.where(valid, leaf, jnp.zeros_like(leaf)) for leaf in grads))
        piece = squares(grads)
        totals = tuple((a + b for a, b in zip(totals, grads)))
        return ((passed, totals), (sent, piece))

    zeros = tuple((jnp.zeros(leaf.shape, jnp.float32) for leaf in weights))
    tick_range = jnp.arange(ticks)
    (unused_grad, totals), (grads_sent, pieces) = lax.scan(
        backward_tick, (start, zeros), tick_range
    )
    flat_sum = lax.psum(flatten_all(totals), "dp")
    summed = split_back(flat_sum, totals)
    input_grads_local = lax.dynamic_slice_in_dim(grads_sent, sections - 1 - section, micro, 0)
    norm_local = lax.dynamic_slice_in_dim(pieces, sections - 1 - section, micro, 0)
    norms = lax.psum(norm_local, "pipe")
    return (
        (outputs_local[None], input_grads_local[None])
        + tuple((leaf[None] for leaf in summed))
        + (norms,)
    )


def solution(mesh):
    in_specs = (
        P("dp", None, None),
        P("dp", None, None),
        P("dp"),
        P("pipe", None),
        P("pipe", None),
        P("pipe", None, None),
        P("pipe", None),
        P("pipe", None, None),
        P("pipe", None),
        P("pipe", None),
        P("pipe", None),
        P("pipe", None, None),
        P("pipe", None),
        P("pipe", None, None),
        P("pipe", None),
    )
    out_specs = (
        P("pipe", "dp", None, None),
        P("pipe", "dp", None, None),
        P("pipe", None),
        P("pipe", None),
        P("pipe", None, None),
        P("pipe", None),
        P("pipe", None, None),
        P("pipe", None),
        P("pipe", None),
        P("pipe", None),
        P("pipe", None, None),
        P("pipe", None),
        P("pipe", None, None),
        P("pipe", None),
        P("dp"),
    )
    return jax.shard_map(
        on_device, mesh=mesh, in_specs=in_specs, out_specs=out_specs, check_vma=False
    )
```

profile of v0, /device:TPU:0, one launch (start us, length us, event | category | flops | bytes accessed | tf_op | source)
XLA Modules:
  0.0 1410.5 jit_solution(10630058524334105209)
XLA Ops:
  10.4 204.8 %while.60 = (s32[]{:T(128)}, bf16[256,768]{1,0:T(8,128)(2,1)S(1)}, bf16[5,256,768]{2,1,0:T(8,128)(2,1)}, bf16[5,256,768]{2,1,0:T(8,128)(2,1)}, pred[]{:T(512)}, ...) while((s32[]{:T(128)}, bf16[256,768]{1,0:T(8,128)(2,1)S(1)}, ...), condition=%wide.region_5.6_spmd.clone.clone.clone, body=%wide.region_0.5_spmd.clone.clone.clone.sunk | while | flops 3891989248 | bytes 53189056 | solution.py:298
  16.9 4.7 convolution_add_fusion.8
  26.0 13.0 fusion.349
  40.3 4.9 collective-permute-start
  45.1 8.3 collective-permute-done
  59.9 4.7 convolution_add_fusion.8
  69.0 13.0 fusion.349
  83.3 4.4 collective-permute-start
  87.7 7.5 collective-permute-done
  101.6 4.7 convolution_add_fusion.8
  110.7 13.0 fusion.349
  125.0 4.4 collective-permute-start
  129.4 6.5 collective-permute-done
  142.3 4.7 convolution_add_fusion.8
  151.4 13.0 fusion.349
  165.7 4.4 collective-permute-start
  170.1 5.6 collective-permute-done
  182.2 4.7 convolution_add_fusion.8
  191.2 13.0 fusion.349
  205.5 4.4 collective-permute-start
  209.9 5.2 collective-permute-done
  217.4 499.0 %while.61 = (s32[]{:T(128)}, bf16[256,768]{1,0:T(8,128)(2,1)}, f32[768]{0:T(1024)}, f32[768]{0:T(1024)}, f32[768,2304]{1,0:T(8,128)}, /*index=5*/f32[2304]{0:T(1...) while((s32[]{:T(128)}, bf16[256,768]{1,0:T(8,128)(2,1)}, ...), condition=%wide.region_34.35_spmd.clone.clone.clone.clone, body=%wide.region_6.34_spmd.clone.clone.clone.clone.sunk | while | flops 10108770304 | bytes 282817472 | solution.py:325
  242.5 4.8 convolution_add_fusion.9
  266.2 4.5 convolution_add_fusion.10
  273.7 3.8 fusion.383
  284.8 7.3 multiply_reduce_fusion.29
  292.1 11.2 multiply_reduce_fusion.37
  303.4 6.7 multiply_reduce_fusion.35
  334.4 4.8 convolution_add_fusion.9
  358.2 4.5 convolution_add_fusion.10
  365.7 3.8 fusion.383
  377.5 9.4 multiply_reduce_fusion.29
  386.9 13.0 multiply_reduce_fusion.37
  400.0 8.2 multiply_reduce_fusion.35
  432.4 4.8 convolution_add_fusion.9
  456.2 4.5 convolution_add_fusion.10
  475.5 9.4 multiply_reduce_fusion.29
  484.9 13.0 multiply_reduce_fusion.37
  497.9 8.2 multiply_reduce_fusion.35
  530.4 4.8 convolution_add_fusion.9
  554.1 4.5 convolution_add_fusion.10
  561.6 3.8 fusion.383
  573.5 9.4 multiply_reduce_fusion.29
  582.8 13.0 multiply_reduce_fusion.37
  595.9 8.2 multiply_reduce_fusion.35
  628.3 4.8 convolution_add_fusion.9
  652.1 4.5 convolution_add_fusion.10
  671.4 9.4 multiply_reduce_fusion.29
  680.8 13.0 multiply_reduce_fusion.37
  693.8 8.2 multiply_reduce_fusion.35
  718.7 7.9 reshape.317
  726.6 9.5 copy.64
  736.2 10.7 reshape.320
  749.5 60.7 %dynamic-update-slice.2 = f32[7087872]{0:T(1024)} dynamic-update-slice(f32[7087872]{0:T(1024)} %constant_dynamic-update-slice_fusion.8, f32[1769472]{0:T(1024)} %reshape.317, s32[]{} %constant.326) | dynamic-update-slice | bytes 14155780
  811.5 20.3 %dynamic-update-slice.4 = f32[7087872]{0:T(1024)} dynamic-update-slice(f32[7087872]{0:T(1024)} %constant_dynamic-update-slice_fusion.7, f32[589824]{0:T(1024)S(1)} %reshape.318, s32[]{} %constant.328) | dynamic-update-slice | bytes 4718596
  835.7 9.3 constant_dynamic-update-slice_fusion.3
  845.6 4.0 constant_dynamic-update-slice_fusion.1
  850.9 9.2 psum.15
  863.6 479.5 %all-reduce.2.cloned.1.call-done = f32[7087872]{0:T(1024)} async-done(((f32[7087872]{0:T(1024)}), f32[7087872]{0:T(1024)}) %all-reduce.2.cloned.1.call-update) | async-done | bytes 28351504 | tf_op jit(solution)/shard_map/psum | solution.py:328
  1352.1 14.2 %fusion.263 = (f32[2359296]{0:T(1024)}, f32[2359296]{0:T(1024)}) fusion(f32[7087872]{0:T(1024)} %all-reduce.2.cloned.1.call-done), kind=kLoop, calls=%fused_computation.377 | loop fusion | bytes 37748736 | tf_op jit(solution)/shard_map/slice | solution.py:49
  1366.4 11.3 broadcast_in_dim_reshape.15
  1377.6 5.2 slice.254
  1382.8 8.2 broadcast_in_dim_reshape.12
  1391.1 10.9 broadcast_in_dim_reshape.14
  (1180 shorter events, 316.8 us)
Async XLA Ops:
  7.3 1335.8 %all-reduce.2.cloned.1.call-start = ((), (), s32[]{:S(2)}) async-start(), calls=%async_computation | async-start | bytes 56705024 | tf_op jit(solution)/shard_map/psum | solution.py:328
  40.3 13.2 collective-permute-start
  83.3 11.9 collective-permute-start
  125.0 10.9 collective-permute-start
  165.7 10.0 collective-permute-start
  205.5 9.7 collective-permute-start
  232.3 15.0 %copy-start.15 = (f32[1,2304]{1,0:T(1,128)}, f32[1,2304]{1,0:T(1,128)S(1)}, u32[]{:S(2)}) copy-start(f32[1,2304]{1,0:T(1,128)S(1)} %get-tuple-element.1934) | copy-start | bytes 27652 | tf_op jit(solution)/shard_map/while
  232.3 15.0 %copy-start.66 = (f32[8]{0:T(128)}, f32[8]{0:T(128)S(1)}, u32[]{:S(2)}) copy-start(f32[8]{0:T(128)S(1)} %get-tuple-element.1941) | copy-start | bytes 100 | tf_op jit(solution)/shard_map/while
  232.3 15.0 %copy-start.71 = (s32[4]{0:T(128)}, s32[4]{0:T(128)S(1)}, u32[]{:S(2)}) copy-start(s32[4]{0:T(128)S(1)} %get-tuple-element.1927) | copy-start | bytes 52 | tf_op jit(solution)/shard_map/while
  232.3 15.0 %copy-start.73 = (s32[5]{0:T(128)}, s32[5]{0:T(128)S(1)}, u32[]{:S(2)}) copy-start(s32[5]{0:T(128)S(1)} %get-tuple-element.1925) | copy-start | bytes 64 | tf_op jit(solution)/shard_map/while
  232.3 27.2 %copy-start.40 = (f32[1,768]{1,0:T(1,128)}, f32[1,768]{1,0:T(1,128)S(1)}, u32[]{:S(2)}) copy-start(f32[1,768]{1,0:T(1,128)S(1)} %get-tuple-element.1937) | copy-start | bytes 9220 | tf_op jit(solution)/shard_map/while
  280.0 43.6 %collective-permute-start.1 = (bf16[256,768]{1,0:T(8,128)(2,1)}, bf16[256,768]{1,0:T(8,128)(2,1)}, u32[]{:S(2)}, u32[]{:S(2)}) collective-permute-start(bf16[256,768]{1,0:T(8,128)(2,1)} %get-tuple-element.1718), channel_id=1, source_target_pairs={{16,0},{17,1},{18,2},{19,3},{20,4},{21,5},{22,6},{23,7},{24,8},{25... | collective-permute-start | bytes 1179656 | tf_op jit(solution)/shard_map/while/body/eval_jaxpr/ppermute | solution.py:21
  310.2 14.0 copy-start.16
  310.2 14.0 copy-start.35
  310.2 14.0 copy-start.38
  310.2 14.0 copy-start.41
  324.3 15.0 %copy-start.15 = (f32[1,2304]{1,0:T(1,128)}, f32[1,2304]{1,0:T(1,128)S(1)}, u32[]{:S(2)}) copy-start(f32[1,2304]{1,0:T(1,128)S(1)} %get-tuple-element.1934) | copy-start | bytes 27652 | tf_op jit(solution)/shard_map/while
  324.3 15.0 %copy-start.66 = (f32[8]{0:T(128)}, f32[8]{0:T(128)S(1)}, u32[]{:S(2)}) copy-start(f32[8]{0:T(128)S(1)} %get-tuple-element.1941) | copy-start | bytes 100 | tf_op jit(solution)/shard_map/while
  324.3 15.0 %copy-start.71 = (s32[4]{0:T(128)}, s32[4]{0:T(128)S(1)}, u32[]{:S(2)}) copy-start(s32[4]{0:T(128)S(1)} %get-tuple-element.1927) | copy-start | bytes 52 | tf_op jit(solution)/shard_map/while
  324.3 15.0 %copy-start.73 = (s32[5]{0:T(128)}, s32[5]{0:T(128)S(1)}, u32[]{:S(2)}) copy-start(s32[5]{0:T(128)S(1)} %get-tuple-element.1925) | copy-start | bytes 64 | tf_op jit(solution)/shard_map/while
  324.3 27.2 %copy-start.40 = (f32[1,768]{1,0:T(1,128)}, f32[1,768]{1,0:T(1,128)S(1)}, u32[]{:S(2)}) copy-start(f32[1,768]{1,0:T(1,128)S(1)} %get-tuple-element.1937) | copy-start | bytes 9220 | tf_op jit(solution)/shard_map/while
  371.9 49.6 %collective-permute-start.1 = (bf16[256,768]{1,0:T(8,128)(2,1)}, bf16[256,768]{1,0:T(8,128)(2,1)}, u32[]{:S(2)}, u32[]{:S(2)}) collective-permute-start(bf16[256,768]{1,0:T(8,128)(2,1)} %get-tuple-element.1718), channel_id=1, source_target_pairs={{16,0},{17,1},{18,2},{19,3},{20,4},{21,5},{22,6},{23,7},{24,8},{25... | collective-permute-start | bytes 1179656 | tf_op jit(solution)/shard_map/while/body/eval_jaxpr/ppermute | solution.py:21
  408.2 14.0 copy-start.16
  408.2 14.0 copy-start.35
  408.2 14.0 copy-start.38
  408.2 14.0 copy-start.41
  408.2 14.0 copy-start.67
  408.2 14.0 copy-start.72
  408.2 14.0 copy-start.74
  422.3 15.0 %copy-start.15 = (f32[1,2304]{1,0:T(1,128)}, f32[1,2304]{1,0:T(1,128)S(1)}, u32[]{:S(2)}) copy-start(f32[1,2304]{1,0:T(1,128)S(1)} %get-tuple-element.1934) | copy-start | bytes 27652 | tf_op jit(solution)/shard_map/while
  422.3 15.0 %copy-start.66 = (f32[8]{0:T(128)}, f32[8]{0:T(128)S(1)}, u32[]{:S(2)}) copy-start(f32[8]{0:T(128)S(1)} %get-tuple-element.1941) | copy-start | bytes 100 | tf_op jit(solution)/shard_map/while
  422.3 15.0 %copy-start.71 = (s32[4]{0:T(128)}, s32[4]{0:T(128)S(1)}, u32[]{:S(2)}) copy-start(s32[4]{0:T(128)S(1)} %get-tuple-element.1927) | copy-start | bytes 52 | tf_op jit(solution)/shard_map/while
  422.3 15.0 %copy-start.73 = (s32[5]{0:T(128)}, s32[5]{0:T(128)S(1)}, u32[]{:S(2)}) copy-start(s32[5]{0:T(128)S(1)} %get-tuple-element.1925) | copy-start | bytes 64 | tf_op jit(solution)/shard_map/while
  422.3 27.2 %copy-start.40 = (f32[1,768]{1,0:T(1,128)}, f32[1,768]{1,0:T(1,128)S(1)}, u32[]{:S(2)}) copy-start(f32[1,768]{1,0:T(1,128)S(1)} %get-tuple-element.1937) | copy-start | bytes 9220 | tf_op jit(solution)/shard_map/while
  469.9 49.6 %collective-permute-start.1 = (bf16[256,768]{1,0:T(8,128)(2,1)}, bf16[256,768]{1,0:T(8,128)(2,1)}, u32[]{:S(2)}, u32[]{:S(2)}) collective-permute-start(bf16[256,768]{1,0:T(8,128)(2,1)} %get-tuple-element.1718), channel_id=1, source_target_pairs={{16,0},{17,1},{18,2},{19,3},{20,4},{21,5},{22,6},{23,7},{24,8},{25... | collective-permute-start | bytes 1179656 | tf_op jit(solution)/shard_map/while/body/eval_jaxpr/ppermute | solution.py:21
  506.1 14.0 copy-start.16
  506.1 14.0 copy-start.35
  506.1 14.0 copy-start.38
  506.2 14.0 copy-start.41
  520.2 15.0 %copy-start.15 = (f32[1,2304]{1,0:T(1,128)}, f32[1,2304]{1,0:T(1,128)S(1)}, u32[]{:S(2)}) copy-start(f32[1,2304]{1,0:T(1,128)S(1)} %get-tuple-element.1934) | copy-start | bytes 27652 | tf_op jit(solution)/shard_map/while
  520.2 15.0 %copy-start.66 = (f32[8]{0:T(128)}, f32[8]{0:T(128)S(1)}, u32[]{:S(2)}) copy-start(f32[8]{0:T(128)S(1)} %get-tuple-element.1941) | copy-start | bytes 100 | tf_op jit(solution)/shard_map/while
  520.2 15.0 %copy-start.71 = (s32[4]{0:T(128)}, s32[4]{0:T(128)S(1)}, u32[]{:S(2)}) copy-start(s32[4]{0:T(128)S(1)} %get-tuple-element.1927) | copy-start | bytes 52 | tf_op jit(solution)/shard_map/while
  520.3 15.0 %copy-start.73 = (s32[5]{0:T(128)}, s32[5]{0:T(128)S(1)}, u32[]{:S(2)}) copy-start(s32[5]{0:T(128)S(1)} %get-tuple-element.1925) | copy-start | bytes 64 | tf_op jit(solution)/shard_map/while
  520.3 27.2 %copy-start.40 = (f32[1,768]{1,0:T(1,128)}, f32[1,768]{1,0:T(1,128)S(1)}, u32[]{:S(2)}) copy-start(f32[1,768]{1,0:T(1,128)S(1)} %get-tuple-element.1937) | copy-start | bytes 9220 | tf_op jit(solution)/shard_map/while
  567.9 49.6 %collective-permute-start.1 = (bf16[256,768]{1,0:T(8,128)(2,1)}, bf16[256,768]{1,0:T(8,128)(2,1)}, u32[]{:S(2)}, u32[]{:S(2)}) collective-permute-start(bf16[256,768]{1,0:T(8,128)(2,1)} %get-tuple-element.1718), channel_id=1, source_target_pairs={{16,0},{17,1},{18,2},{19,3},{20,4},{21,5},{22,6},{23,7},{24,8},{25... | collective-permute-start | bytes 1179656 | tf_op jit(solution)/shard_map/while/body/eval_jaxpr/ppermute | solution.py:21
  604.1 14.0 copy-start.16
  604.1 14.0 copy-start.35
  604.1 14.0 copy-start.38
  604.1 14.0 copy-start.41
  618.2 15.0 %copy-start.15 = (f32[1,2304]{1,0:T(1,128)}, f32[1,2304]{1,0:T(1,128)S(1)}, u32[]{:S(2)}) copy-start(f32[1,2304]{1,0:T(1,128)S(1)} %get-tuple-element.1934) | copy-start | bytes 27652 | tf_op jit(solution)/shard_map/while
  618.2 15.0 %copy-start.66 = (f32[8]{0:T(128)}, f32[8]{0:T(128)S(1)}, u32[]{:S(2)}) copy-start(f32[8]{0:T(128)S(1)} %get-tuple-element.1941) | copy-start | bytes 100 | tf_op jit(solution)/shard_map/while
  618.2 15.0 %copy-start.71 = (s32[4]{0:T(128)}, s32[4]{0:T(128)S(1)}, u32[]{:S(2)}) copy-start(s32[4]{0:T(128)S(1)} %get-tuple-element.1927) | copy-start | bytes 52 | tf_op jit(solution)/shard_map/while
  618.2 15.0 %copy-start.73 = (s32[5]{0:T(128)}, s32[5]{0:T(128)S(1)}, u32[]{:S(2)}) copy-start(s32[5]{0:T(128)S(1)} %get-tuple-element.1925) | copy-start | bytes 64 | tf_op jit(solution)/shard_map/while
  618.2 27.2 %copy-start.40 = (f32[1,768]{1,0:T(1,128)}, f32[1,768]{1,0:T(1,128)S(1)}, u32[]{:S(2)}) copy-start(f32[1,768]{1,0:T(1,128)S(1)} %get-tuple-element.1937) | copy-start | bytes 9220 | tf_op jit(solution)/shard_map/while
  665.8 49.6 %collective-permute-start.1 = (bf16[256,768]{1,0:T(8,128)(2,1)}, bf16[256,768]{1,0:T(8,128)(2,1)}, u32[]{:S(2)}, u32[]{:S(2)}) collective-permute-start(bf16[256,768]{1,0:T(8,128)(2,1)} %get-tuple-element.1718), channel_id=1, source_target_pairs={{16,0},{17,1},{18,2},{19,3},{20,4},{21,5},{22,6},{23,7},{24,8},{25... | collective-permute-start | bytes 1179656 | tf_op jit(solution)/shard_map/while/body/eval_jaxpr/ppermute | solution.py:21
  702.0 14.0 copy-start.16
  702.1 14.0 copy-start.35
  702.1 14.0 copy-start.38
  702.1 14.0 copy-start.41
  702.1 14.0 copy-start.67
  749.5 60.7 %copy-start.29 = (f32[2304]{0:T(1024)S(1)}, f32[2304]{0:T(1024)}, u32[]{:S(2)}) copy-start(f32[2304]{0:T(1024)} %get-tuple-element.535) | copy-start | bytes 27652
  810.2 21.6 %copy-start.59 = (f32[768]{0:T(1024)S(1)}, f32[768]{0:T(1024)}, u32[]{:S(2)}) copy-start(f32[768]{0:T(1024)} %get-tuple-element.537) | copy-start | bytes 9220
  810.2 22.9 %copy-start.47 = (f32[768]{0:T(1024)S(1)}, f32[768]{0:T(1024)}, u32[]{:S(2)}) copy-start(f32[768]{0:T(1024)} %get-tuple-element.538) | copy-start | bytes 9220
  810.2 24.2 %copy-start.44 = (f32[768]{0:T(1024)S(1)}, f32[768]{0:T(1024)}, u32[]{:S(2)}) copy-start(f32[768]{0:T(1024)} %get-tuple-element.539) | copy-start | bytes 9220
  (302 other events, 2194.7 us)
Sparse Core Ops, SparseCore 0:
  850.3 492.7 all-reduce.1
where the time goes:
time: 1430 us; the launch traced here: 1410 us
  waiting for transfers between devices  513 us (36%)
  matrix products  400 us (28%)
  local copies, waits for them, and re-layouts  265 us (19%)
  other arithmetic  111 us (8%)
  loops' own time  69 us (5%)
  starting transfers between devices  28.9 us (2%)
  between operations  14.7 us (1%)
    psum x1, waiting for transfers between devices, on_device(): flat_sum = lax.psum(flatten_all(totals), 'dp')  479 us
    dot_general x20, matrix products, product_tn(): lax.dot_general(left, right, (((0,), (0,)), ((), ())), preferred_element_...  155 us
    dot_general x25, matrix products, product(): return jnp.dot(left, right, preferred_element_type=jnp.float32)  141 us
    unnamed x52, local copies, waits for them, and re-layouts  113 us
    another operation x1, loops' own time, on_device(): lax.scan(backward_tick, (start, zeros), tick_range)  61.7 us
    dot_general x20, matrix products, product_nt(): lax.dot_general(left, right, (((1,), (1,)), ((), ())), preferred_element_...  48.5 us
    ppermute x10, waiting for transfers between devices, passed_along(): return lax.ppermute(array, axis, pairs)  33.2 us
    another operation x4, local copies, waits for them, and re-layouts, on_device(): leaf[None]  32 us
  transfers between devices with their start and end apart: 11, of which 6 were waited for; matrix products, arithmetic and copies ran while one was open for 14% of the time, Pallas kernels for 0%

commit v1 on v0

v1 whole, which is shorter than its diff:
```python
import functools

import jax
import jax.numpy as jnp
import numpy as np
from jax import lax
from jax.experimental import pallas as pl
from jax.experimental.pallas import tpu as pltpu
from jax.sharding import PartitionSpec as P

HEADS = 12
HEAD = 64
ROT = 16
EPSILON = 1e-05
NEG_FILL = -1e30
INV_ROOT_TWO = 0.7071067811865476
INV_ROOT_TWO_PI = 0.3989422804014327
MESH = pl.DeviceIdType.MESH
F32 = jnp.float32
BF16 = jnp.bfloat16


def dot_nn(a, b):
    return jnp.dot(a, b, preferred_element_type=F32)


def dot_nt(a, b):
    return lax.dot_general(a, b, (((1,), (1,)), ((), ())), preferred_element_type=F32)


def dot_tn(a, b):
    return lax.dot_general(a, b, (((0,), (0,)), ((), ())), preferred_element_type=F32)


def rotary_tables(seq):
    half = ROT // 2
    freq = 10000.0 ** (-2.0 * np.arange(half) / ROT)
    angle = np.arange(seq)[:, None] * freq[None, :]
    cosine, sine = np.cos(angle), np.sin(angle)
    own = np.ones((seq, HEAD))
    up = np.zeros((seq, HEAD))
    down = np.zeros((seq, HEAD))
    own[:, :half] = cosine
    own[:, half:ROT] = cosine
    up[:, half:ROT] = sine
    down[:, :half] = -sine
    tables = np.stack([np.concatenate([t, t], axis=1) for t in (own, up, down)])
    return tables.astype(np.float32)


def section_kernel(
    n_mb,
    lens,
    inputs,
    cot,
    g1,
    b1,
    wqkv,
    bqkv,
    wd,
    bd,
    g2,
    b2,
    wi,
    bi,
    wo,
    bo,
    tables,
    out_y,
    out_dx,
    a_hbm,
    b_hbm,
    small,
    wqkv_v,
    wd_v,
    wi_v,
    wo_v,
    xb,
    av,
    bv,
    pb,
    yb,
    dxb,
    acc,
    dctx_v,
    bias_v,
    wsem,
    insem,
    cotsem,
    ysem,
    dxsem,
    asem,
    bsem,
    fsend,
    frecv,
    bsend,
    brecv,
):
    section = lax.axis_index("pipe")
    first = section == 0
    last = section == 1
    peer = 1 - section
    seq, d = xb.shape[1], xb.shape[2]
    pairs = d // 128

    wcopies = [
        pltpu.make_async_copy(src.at[0], dst, wsem.at[k])
        for k, (src, dst) in enumerate(((wqkv, wqkv_v), (wd, wd_v), (wi, wi_v), (wo, wo_v)))
    ]

    @pl.when(first)
    def _():
        pltpu.make_async_copy(inputs, xb, insem).start()

    for c in wcopies:
        c.start()

    @pl.when(last)
    def _():
        pltpu.make_async_copy(cot, bv.at[4], cotsem).start()

    barrier = pltpu.get_barrier_semaphore()
    pl.semaphore_signal(barrier, inc=1, device_id={"pipe": peer}, device_id_type=MESH)
    pl.semaphore_wait(barrier, 1)

    def fcopy(i):
        return pltpu.make_async_remote_copy(
            src_ref=yb.at[i],
            dst_ref=xb.at[i],
            send_sem=fsend.at[i],
            recv_sem=frecv.at[i],
            device_id={"pipe": peer},
            device_id_type=MESH,
        )

    def bcopy(i):
        return pltpu.make_async_remote_copy(
            src_ref=dxb.at[i],
            dst_ref=bv.at[4, i],
            send_sem=bsend.at[i],
            recv_sem=brecv.at[i],
            device_id={"pipe": peer},
            device_id_type=MESH,
        )

    lane = lax.broadcasted_iota(jnp.int32, (seq, 128), 1)
    lower = lane < HEAD

    def pick(value, a):
        return jnp.where(lower if a == 0 else jnp.logical_not(lower), value, jnp.zeros_like(value))

    def rotate(w, sign):
        return (
            w * tables[0]
            + sign * (pltpu.roll(w, ROT // 2, 1) * tables[1] + pltpu.roll(w, 128 - ROT // 2, 1) * tables[2])
        )

    def unit_of(i):
        x = xb[i].astype(F32)
        center = x - jnp.mean(x, axis=-1, keepdims=True)
        inverse = lax.rsqrt(jnp.mean(center * center, axis=-1, keepdims=True) + EPSILON)
        return x, center * inverse, inverse

    def forward(i, carry):
        @pl.when(last)
        def _():
            fcopy(i).wait_recv()

        x, unit, inverse = unit_of(i)
        a1 = (unit * g1[...] + b1[...]).astype(BF16)
        a2 = (unit * g2[...] + b2[...]).astype(BF16)
        av[5, i] = a1
        av[0, i] = a2

        @pl.when(i == 0)
        def _():
            wcopies[0].wait()

        for t in range(3):
            mixed = dot_nn(a1, wqkv_v[:, t * d : (t + 1) * d]) + bqkv[:, t * d : (t + 1) * d]
            if t == 2:
                bv[5 + t, i] = mixed.astype(BF16)
            else:
                for hp in range(pairs):
                    w = rotate(mixed[:, hp * 128 : (hp + 1) * 128], 1.0)
                    if t == 0:
                        w = w * HEAD ** (-0.5)
                    bv[5 + t, i, :, hp * 128 : (hp + 1) * 128] = w.astype(BF16)

        key = lax.broadcasted_iota(jnp.int32, (seq, seq), 0)
        query = lax.broadcasted_iota(jnp.int32, (seq, seq), 1)
        bias_v[...] = jnp.where((key <= query) & (key < lens[i]), 0.0, NEG_FILL)

        def attend(hp, carry):
            cols = pl.ds(pl.multiple_of(hp * 128, 128), 128)
            qp, kp, vp = bv[5, i, :, cols], bv[6, i, :, cols], bv[7, i, :, cols]
            ctx = None
            for a in range(2):
                scores = dot_nt(pick(kp, a), qp) + bias_v[...]
                expo = jnp.exp(scores - jnp.max(scores, axis=0, keepdims=True))
                probs = (expo * (1.0 / jnp.sum(expo, axis=0, keepdims=True))).astype(BF16)
                pb[i, 2 * hp + a] = probs
                part = dot_tn(probs, pick(vp, a))
                ctx = part if ctx is None else ctx + part
            av[6, i, :, cols] = ctx.astype(BF16)
            return carry

        lax.fori_loop(0, pairs, attend, 0)

        @pl.when(i == 0)
        def _():
            for k in (1, 2, 3):
                wcopies[k].wait()

        acc[...] = x + dot_nn(av[6, i], wd_v[...]) + bd[...] + bo[...]

        def feed(j, carry):
            cols = pl.ds(pl.multiple_of(j * d, 128), d)
            hidden = dot_nn(av[0, i], wi_v[:, cols]) + bi[:, cols]
            gate = 0.5 * (1.0 + lax.erf(hidden * INV_ROOT_TWO))
            act = (hidden * gate).astype(BF16)
            av[1 + j, i] = act
            bv[j, i] = (gate + hidden * jnp.exp(-0.5 * hidden * hidden) * INV_ROOT_TWO_PI).astype(BF16)
            acc[...] += dot_nn(act, wo_v[pl.ds(pl.multiple_of(j * d, 128), d), :])
            return carry

        lax.fori_loop(0, 4, feed, 0)
        yb[i] = acc[...].astype(BF16)

        @pl.when(first)
        def _():
            fcopy(i).start()

        pltpu.make_async_copy(yb.at[i], out_y.at[0, i], ysem.at[i]).start()
        for k in range(7):
            pltpu.make_async_copy(av.at[k, i], a_hbm.at[k, i], asem.at[k, i]).start()
        return carry

    def backward(i, carry):
        @pl.when(first)
        def _():
            bcopy(i).wait_recv()

        @pl.when(last)
        def _():
            row = lax.broadcasted_iota(jnp.int32, (seq, d), 0)
            value = bv[4, i].astype(F32)
            bv[4, i] = jnp.where(row < lens[i], value, 0.0).astype(BF16)

        gy = bv[4, i]
        small[i, 7:8, :] = jnp.sum(gy.astype(F32), axis=0, keepdims=True)
        acc[...] = jnp.zeros_like(acc)

        def feed(j, carry):
            cols = pl.ds(pl.multiple_of(j * d, 128), d)
            dact = dot_nt(bv[4, i], wo_v[pl.ds(pl.multiple_of(j * d, 128), d), :])
            dh = (dact * bv[j, i].astype(F32)).astype(BF16)
            bv[j, i] = dh
            small[i, pl.ds(8 + j, 1), :] = jnp.sum(dh.astype(F32), axis=0, keepdims=True)
            acc[...] += dot_nt(dh, wi_v[:, cols])
            return carry

        lax.fori_loop(0, 4, feed, 0)
        dctx_v[...] = dot_nt(gy, wd_v[...]).astype(BF16)

        def attend(hp, carry):
            cols = pl.ds(pl.multiple_of(hp * 128, 128), 128)
            qp, kp, vp = bv[5, i, :, cols], bv[6, i, :, cols], bv[7, i, :, cols]
            dop = dctx_v[:, cols]
            dq = dk = dv = None
            for a in range(2):
                probs = pb[i, 2 * hp + a]
                pf = probs.astype(F32)
                dprob = dot_nt(pick(vp, a), dop)
                prod = dprob * pf
                ds = (prod - pf * jnp.sum(prod, axis=0, keepdims=True)).astype(BF16)
                dv_a = dot_nn(probs, pick(dop, a))
                dk_a = dot_nn(ds, pick(qp, a))
                dq_a = dot_tn(ds, pick(kp, a))
                dv = dv_a if dv is None else dv + dv_a
                dk = dk_a if dk is None else dk + dk_a
                dq = dq_a if dq is None else dq + dq_a
            for t, w in ((0, rotate(dq * HEAD ** (-0.5), -1.0)), (1, rotate(dk, -1.0)), (2, dv)):
                w = w.astype(BF16)
                bv[5 + t, i, :, cols] = w
                small[i, 4 + t : 5 + t, cols] = jnp.sum(w.astype(F32), axis=0, keepdims=True)
            return carry

        lax.fori_loop(0, pairs, attend, 0)
        da1 = dot_nt(bv[5, i], wqkv_v[:, 0:d])
        da1 = da1 + dot_nt(bv[6, i], wqkv_v[:, d : 2 * d])
        da1 = da1 + dot_nt(bv[7, i], wqkv_v[:, 2 * d : 3 * d])
        da2 = acc[...]
        x, unit, inverse = unit_of(i)
        small[i, 0:1, :] = jnp.sum(da1 * unit, axis=0, keepdims=True)
        small[i, 1:2, :] = jnp.sum(da1, axis=0, keepdims=True)
        small[i, 2:3, :] = jnp.sum(da2 * unit, axis=0, keepdims=True)
        small[i, 3:4, :] = jnp.sum(da2, axis=0, keepdims=True)
        scaled = da1 * g1[...] + da2 * g2[...]
        mean_g = jnp.mean(scaled, axis=-1, keepdims=True)
        mean_gn = jnp.mean(scaled * unit, axis=-1, keepdims=True)
        dx = bv[4, i].astype(F32) + inverse * (scaled - mean_g - unit * mean_gn)
        dxb[i] = dx.astype(BF16)

        @pl.when(last)
        def _():
            bcopy(i).start()

        pltpu.make_async_copy(dxb.at[i], out_dx.at[0, i], dxsem.at[i]).start()
        for k in range(8):
            pltpu.make_async_copy(bv.at[k, i], b_hbm.at[k, i], bsem.at[k, i]).start()
        return carry

    @pl.when(first)
    def _():
        pltpu.make_async_copy(inputs, xb, insem).wait()

    lax.fori_loop(0, n_mb, forward, 0)

    @pl.when(last)
    def _():
        pltpu.make_async_copy(cot, bv.at[4], cotsem).wait()

    lax.fori_loop(0, n_mb, backward, 0)

    def drain(i, carry):
        @pl.when(first)
        def _():
            fcopy(i).wait_send()

        @pl.when(last)
        def _():
            bcopy(i).wait_send()

        pltpu.make_async_copy(yb.at[i], out_y.at[0, i], ysem.at[i]).wait()
        pltpu.make_async_copy(dxb.at[i], out_dx.at[0, i], dxsem.at[i]).wait()
        for k in range(7):
            pltpu.make_async_copy(av.at[k, i], a_hbm.at[k, i], asem.at[k, i]).wait()
        for k in range(8):
            pltpu.make_async_copy(bv.at[k, i], b_hbm.at[k, i], bsem.at[k, i]).wait()
        return carry

    lax.fori_loop(0, n_mb, drain, 0)


def section_call(lens, inputs, cot, params, tables):
    n_mb, seq, d = inputs.shape
    g1, b1, wqkv, bqkv, wd, bd, g2, b2, wi, bi, wo, bo = params
    ff = wi.shape[2]
    vmem = pl.BlockSpec(memory_space=pltpu.VMEM)
    smem = pl.BlockSpec(memory_space=pltpu.SMEM)
    hbm = pl.BlockSpec(memory_space=pl.ANY)
    dma = pltpu.SemaphoreType.DMA
    flops = n_mb * 2 * seq * (3 * d * d + d * d + 2 * d * ff) * 2
    return pl.pallas_call(
        functools.partial(section_kernel, n_mb),
        out_shape=(
            jax.ShapeDtypeStruct((1, n_mb, seq, d), BF16),
            jax.ShapeDtypeStruct((1, n_mb, seq, d), BF16),
            jax.ShapeDtypeStruct((7, n_mb, seq, d), BF16),
            jax.ShapeDtypeStruct((8, n_mb, seq, d), BF16),
            jax.ShapeDtypeStruct((n_mb, 16, d), F32),
        ),
        in_specs=[smem, hbm, hbm, vmem, vmem, hbm, vmem, hbm, vmem, vmem, vmem, hbm, vmem, hbm, vmem, vmem],
        out_specs=(hbm, hbm, hbm, hbm, vmem),
        scratch_shapes=[
            pltpu.VMEM((d, 3 * d), BF16),
            pltpu.VMEM((d, d), BF16),
            pltpu.VMEM((d, ff), BF16),
            pltpu.VMEM((ff, d), BF16),
            pltpu.VMEM((n_mb, seq, d), BF16),
            pltpu.VMEM((7, n_mb, seq, d), BF16),
            pltpu.VMEM((8, n_mb, seq, d), BF16),
            pltpu.VMEM((n_mb, HEADS, seq, seq), BF16),
            pltpu.VMEM((n_mb, seq, d), BF16),
            pltpu.VMEM((n_mb, seq, d), BF16),
            pltpu.VMEM((seq, d), F32),
            pltpu.VMEM((seq, d), BF16),
            pltpu.VMEM((seq, seq), F32),
            dma((4,)),
            dma,
            dma,
            dma((n_mb,)),
            dma((n_mb,)),
            dma((7, n_mb)),
            dma((8, n_mb)),
            dma((n_mb,)),
            dma((n_mb,)),
            dma((n_mb,)),
            dma((n_mb,)),
        ],
        compiler_params=pltpu.CompilerParams(
            collective_id=0, has_side_effects=True, vmem_limit_bytes=62 * 2**20
        ),
        cost_estimate=pl.CostEstimate(flops=flops, bytes_accessed=40 * 2**20, transcendentals=0),
    )(lens, inputs, cot, g1, b1, wqkv, bqkv, wd, bd, g2, b2, wi, bi, wo, bo, tables)


def a_index(b):
    return jnp.where(b < 4, 0, jnp.where(b < 8, b - 3, jnp.where(b < 11, 5, 6)))


def b_index(b):
    return jnp.where(b < 4, b, jnp.where(b < 8, 4, jnp.where(b < 11, b - 3, 4)))


def weight_kernel(a_ref, b_ref, p_ref, nrm_ref):
    n_mb, seq, d = a_ref.shape[1:]

    @pl.when(pl.program_id(0) == 0)
    def _():
        nrm_ref[...] = jnp.zeros_like(nrm_ref)

    step = 256
    for c in range(d // step):
        cols = slice(c * step, (c + 1) * step)
        total = None
        for m in range(n_mb):
            grad = dot_tn(a_ref[0, m], b_ref[0, m, :, cols])
            squares = jnp.sum((grad * grad).reshape(d // 8, 8, step), axis=0)
            nrm_ref[m] += squares[:, :128] + squares[:, 128:]
            total = grad if total is None else total + grad
        p_ref[0, :, cols] = total.astype(BF16)


def weight_call(a, b):
    n_mb, seq, d = a.shape[1:]
    return pl.pallas_call(
        weight_kernel,
        grid=(12,),
        out_shape=(
            jax.ShapeDtypeStruct((12, d, d), BF16),
            jax.ShapeDtypeStruct((n_mb, 8, 128), F32),
        ),
        in_specs=[
            pl.BlockSpec((1, n_mb, seq, d), lambda g: (a_index(g), 0, 0, 0)),
            pl.BlockSpec((1, n_mb, seq, d), lambda g: (b_index(g), 0, 0, 0)),
        ],
        out_specs=(
            pl.BlockSpec((1, d, d), lambda g: (g, 0, 0)),
            pl.BlockSpec((n_mb, 8, 128), lambda g: (0, 0, 0)),
        ),
        compiler_params=pltpu.CompilerParams(vmem_limit_bytes=48 * 2**20),
        cost_estimate=pl.CostEstimate(
            flops=12 * 2 * n_mb * seq * d * d, bytes_accessed=40 * 2**20, transcendentals=0
        ),
    )(a, b)


def on_device(inputs, cotangent, lengths, *params):
    n_mb, seq, d = inputs.shape
    tables = jnp.asarray(rotary_tables(seq))
    out_y, out_dx, a, b, small = section_call(lengths, inputs, cotangent, params, tables)
    partial, nrm = weight_call(a, b)
    small = small[:, :12]
    weight = jnp.ones((12, 1), F32).at[7].set(2.0)
    norms = jnp.sum(nrm, axis=(1, 2)) + jnp.sum(small * small * weight, axis=(1, 2))
    norms = lax.psum(norms, "pipe")
    summed = lax.psum(partial, "dp").astype(F32)
    vectors = lax.psum(jnp.sum(small, axis=0), "dp")
    rows = [vectors[k : k + 1] for k in range(12)]
    w_in = jnp.concatenate([summed[k] for k in range(4)], axis=1)[None]
    w_out = summed[4:8].reshape(1, 4 * d, d)
    w_qkv = jnp.concatenate([summed[8 + k] for k in range(3)], axis=1)[None]
    w_dense = summed[11:12]
    return (
        out_y,
        out_dx,
        rows[0],
        rows[1],
        w_qkv,
        vectors[4:7].reshape(1, 3 * d),
        w_dense,
        rows[7],
        rows[2],
        rows[3],
        w_in,
        vectors[8:12].reshape(1, 4 * d),
        w_out,
        rows[7],
        norms,
    )


def solution(mesh):
    matrix, vector = P("pipe", None, None), P("pipe", None)
    weights = (vector, vector, matrix, vector, matrix, vector) * 2
    tokens = P("dp", None, None)
    return jax.shard_map(
        on_device,
        mesh=mesh,
        in_specs=(tokens, tokens, P("dp")) + weights,
        out_specs=(P("pipe", "dp", None, None),) * 2 + weights + (P("dp"),),
        check_vma=False,
    )
```

time: 1430 us -> 472 us (0.33); the launches traced: 1410 us -> 472 us
  matrix products: 400 us -> 0 us
  waiting for transfers between devices: 513 us -> 187 us
  local copies, waits for them, and re-layouts: 265 us -> 20.4 us
  Pallas kernels: 0 us -> 157 us
  other arithmetic: 111 us -> 24.9 us
  loops' own time: 69 us -> 0 us
  blocking collectives: 9.16 us -> 68.4 us
  starting transfers between devices: 28.9 us -> 0.04 us
    dot_general x105 -> x0, matrix products: 400 us -> none  [the longest x20 155 us: product_tn(): lax.dot_general(left, right, (((0,), (0,)), ((), ())), preferred_element_...]
    psum x1, waiting for transfers between devices: 479 us -> 187 us  [on_device(): summed = lax.psum(partial, 'dp').astype(F32)]
    pallas_call x0 -> x2, Pallas kernels: none -> 157 us  [the longest x1 133 us: section_call(): pl.pallas_call(functools.partial(section_kernel, n_mb), out_shape=(jax.Sh...]
    unnamed x52 -> x25, local copies, waits for them, and re-layouts: 113 us -> 7.07 us
    another operation x2 -> x0, loops' own time: 69 us -> none  [the longest x1 61.7 us: on_device(): lax.scan(backward_tick, (start, zeros), tick_range)]
    psum x1 -> x2, blocking collectives: 9.16 us -> 68.4 us  [the longest x1 62.9 us: on_device(): vectors = lax.psum(jnp.sum(small, axis=0), 'dp')]
    reduce_sum x65 -> x2, other arithmetic: 51.3 us -> 0.29 us  [the longest x1 0.18 us: on_device(): jnp.sum(small * small * weight, axis=(1, 2))]
    another operation x9 -> x0, local copies, waits for them, and re-layouts: 37.1 us -> none  [the longest x4 32 us: on_device(): leaf[None]]
  transfers between devices with their start and end apart: 11 -> 1, of which waited for: 6 -> 1; matrix products, arithmetic and copies ran while one was open for 14% -> 0% of each run, Pallas kernels for 0% -> 0%
where the time goes in v1:
time: 472 us
  waiting for transfers between devices  187 us (40%)
  Pallas kernels  157 us (33%)
  blocking collectives  68.4 us (14%)
  other arithmetic  24.9 us (5%)
  local copies, waits for them, and re-layouts  20.4 us (4%)
  between operations  14.1 us (3%)
    psum x1, waiting for transfers between devices, on_device(): summed = lax.psum(partial, 'dp').astype(F32)  187 us
    pallas_call x1, Pallas kernels, section_call(): pl.pallas_call(functools.partial(section_kernel, n_mb), out_shape=(jax.Sh...  133 us
    psum x1, blocking collectives, on_device(): vectors = lax.psum(jnp.sum(small, axis=0), 'dp')  62.9 us
    pallas_call x1, Pallas kernels, weight_call(): pl.pallas_call(weight_kernel, grid=(12,), out_shape=(jax.ShapeDtypeStruct...  24 us
    convert_element_type x1, other arithmetic, on_device(): summed = lax.psum(partial, 'dp').astype(F32)  15.7 us
  transfers between devices with their start and end apart: 1, of which 1 were waited for; matrix products, arithmetic and copies ran while one was open for 0% of the time, Pallas kernels for 0%

profile of v1, /device:TPU:0, one launch (start us, length us, event | category | flops | bytes accessed | tf_op | source)
XLA Modules:
  0.0 471.7 jit_solution(12684695615824700515)
XLA Ops:
  7.2 0.0 all-reduce.2.cloned.1.call-start
  7.2 133.4 %shard_map.271 = (bf16[1,4,256,768]{3,2,1,0:T(8,128)(2,1)}, bf16[1,4,256,768]{3,2,1,0:T(8,128)(2,1)}, bf16[7,4,256,768]{3,2,1,0:T(8,128)(2,1)}, bf16[8,4,256,768]{3,2,1,0:T(8,128)(2,1)}, f32[4,16,768]{2,1,0:T(8,128)}) custom-call(s32[4]{0:T(128)} %lens.1, bf16[4,256,768]{2,1,0:T(8,128)(2,1)} %inputs.1, bf16[4,256,768]{2,1,0:T(8,128)(2,1)} %cot.1, ...), custom_call_target="tpu_custom_call" | custom-call | flops 28991029248 | bytes 41943040 | tf_op jit(solution)/shard_map/pallas_call | solution.py:355
  140.6 24.0 %shard_map.272 = (bf16[12,768,768]{2,1,0:T(8,128)(2,1)}, f32[4,8,128]{2,1,0:T(8,128)S(1)}) custom-call(bf16[7,4,256,768]{3,2,1,0:T(8,128)(2,1)} %get-tuple-element.37.a_ref, bf16[8,4,256,768]{3,2,1,0:T(8,128)(2,1)} %get-tuple-element.38.b_ref), custom_call_target="tpu_custom_call" | custom-call | flops 14495514624 | bytes 41943040 | tf_op jit(solution)/shard_map/pallas_call | solution.py:428
  164.6 0.0 copy-start.2
  164.6 0.0 copy-start.4
  164.6 0.0 all-reduce.2.cloned.1.call-update
  164.6 0.1 reduce_sum.28
  164.7 0.8 copy-done.2
  165.5 0.0 copy-done.4
  165.5 0.2 multiply_reduce_fusion
  165.7 5.4 %psum.23 = f32[4]{0:T(128)} all-reduce(f32[4]{0:T(128)S(1)} %add.11), channel_id=1, replica_groups=mesh['pipe'=2,'dp'=16] {'pipe'}, use_global_device_ids=true, to_apply=%region_5.0 | all-reduce | flops 4 | bytes 32 | tf_op jit(solution)/shard_map/psum | solution.py:458
  171.2 62.9 %psum.21 = f32[12,768]{1,0:T(8,128)S(1)} all-reduce(f32[12,768]{1,0:T(8,128)S(1)} %get-tuple-element.42), channel_id=1, replica_groups=mesh['pipe'=2,'dp'=16] {'dp'}, use_global_device_ids=true, to_apply=%region_1.0 | all-reduce | flops 9216 | bytes 73728 | tf_op jit(solution)/shard_map/psum | solution.py:460
  234.1 0.6 copy.31
  234.7 0.6 copy.32
  235.3 0.6 fusion
  235.9 0.0 copy-start.3
  235.9 186.5 %all-reduce.2.cloned.1.call-done = bf16[12,768,768]{2,1,0:T(8,128)(2,1)} async-done(((bf16[12,768,768]{2,1,0:T(8,128)(2,1)}), bf16[12,768,768]{2,1,0:T(8,128)(2,1)}) %all-reduce.2.cloned.1.call-update) | async-done | bytes 14155792 | tf_op jit(solution)/shard_map/psum | solution.py:459
  422.5 15.7 %convert_element_type.3 = f32[12,768,768]{2,1,0:T(8,128)} convert(bf16[12,768,768]{2,1,0:T(8,128)(2,1)} %all-reduce.2.cloned.1.call-done) | non-fusion elementwise | flops 7077888 | bytes 42467328 | tf_op jit(solution)/shard_map/convert_element_type | solution.py:459
  438.2 6.6 %slice_bitcast_fusion.3 = (f32[768,768]{1,0:T(8,128)S(1)}, f32[768,768]{1,0:T(8,128)S(1)}, f32[768,768]{1,0:T(8,128)S(1)}, f32[768,768]{1,0:T(8,128)S(1)}, f32[7...) fusion(f32[12,768,768]{2,1,0:T(8,128)} %convert_element_type.3), kind=kLoop, calls=%fused_computation.5 | loop fusion | bytes 33030144 | tf_op jit(solution)/shard_map/squeeze | solution.py:462
  444.7 0.0 slice-start
  444.8 0.0 slice-start.1
  444.8 3.8 maximum_bitcast_fusion.1
  448.6 0.0 slice-start.2
  448.6 0.0 slice-start.3
  448.6 5.1 %maximum_bitcast_fusion = f32[1,768,3072]{2,1,0:T(8,128)} fusion(f32[768,768]{1,0:T(8,128)S(1)} %get-tuple-element.46, f32[768,768]{1,0:T(8,128)S(1)} %get-tuple-element.44, f32[768,768]{1,0:T(8,128)S(1)} %get-tuple-element.45, f32[768,768]{1,0:T(8,128)S(1)} %get-tuple-element.43), kind=kLoop, calls=%fused_computation | loop fusion | flops 7077888 | bytes 18874368 | tf_op jit(solution)/shard_map/broadcast_in_dim | solution.py:462
  453.7 0.0 slice-done
  453.7 0.0 slice-done.1
  453.7 1.8 slice-done.2
  455.5 0.4 slice-done.3
  455.9 1.6 slice.88
  457.4 0.0 copy-start.1
  457.4 4.6 slice.97
  462.0 0.0 copy-start
  462.0 0.0 copy-done.3
  462.0 0.6 copy.37
  462.6 0.0 copy-done.1
  462.6 1.1 copy.38
  463.7 0.0 copy-done
  463.7 1.1 copy.39
  (4 shorter events, 0.0 us)
Async XLA Ops:
  7.2 415.3 %all-reduce.2.cloned.1.call-start = ((), (), s32[]{:S(2)}) async-start(), calls=%async_computation | async-start | bytes 28311552 | tf_op jit(solution)/shard_map/psum | solution.py:459
  164.6 0.9 copy-start.2
  164.6 0.9 copy-start.4
  235.9 226.1 %copy-start.3 = (f32[1,768]{1,0:T(1,128)}, f32[1,768]{1,0:T(1,128)S(1)}, u32[]{:S(2)}) copy-start(f32[1,768]{1,0:T(1,128)S(1)} %get-tuple-element.107) | copy-start | bytes 9220
  444.7 8.9 %slice-start = ((s8[14155776]{0:T(1024)(128)(4,1)}), s8[4194304]{0:T(1024)(128)(4,1)S(1)}, s32[]{:S(2)}) async-start(s8[14155776]{0:T(1024)(128)(4,1)} %bitcast.27), calls=%async_computation.1 | async-start | bytes 8388608
  444.8 8.9 %slice-start.1 = ((s8[14155776]{0:T(1024)(128)(4,1)}), s8[4194304]{0:T(1024)(128)(4,1)S(1)}, s32[]{:S(2)}) async-start(s8[14155776]{0:T(1024)(128)(4,1)} %bitcast.27), calls=%async_computation.2 | async-start | bytes 8388608
  448.6 6.8 %slice-start.2 = ((s8[14155776]{0:T(1024)(128)(4,1)}), s8[4194304]{0:T(1024)(128)(4,1)S(1)}, s32[]{:S(2)}) async-start(s8[14155776]{0:T(1024)(128)(4,1)} %bitcast.27), calls=%async_computation.3 | async-start | bytes 8388608
  448.6 7.2 %slice-start.3 = ((s8[14155776]{0:T(1024)(128)(4,1)}), s8[1572864]{0:T(1024)(128)(4,1)S(1)}, s32[]{:S(2)}) async-start(s8[14155776]{0:T(1024)(128)(4,1)} %bitcast.27), calls=%async_computation.4 | async-start | bytes 3145728
  457.4 5.2 %copy-start.1 = (bf16[1,4,256,768]{3,2,1,0:T(8,128)(2,1)S(1)}, bf16[1,4,256,768]{3,2,1,0:T(8,128)(2,1)}, u32[]{:S(2)}) copy-start(bf16[1,4,256,768]{3,2,1,0:T(8,128)(2,1)} %get-tuple-element.100) | copy-start | bytes 4718596
  462.0 1.7 copy-start
Sparse Core Ops, SparseCore 0:
  164.7 257.6 all-reduce.1

commit v2 on v1

--- a/solution.py
+++ b/solution.py
@@ -396,87 +396,507 @@
     )(lens, inputs, cot, g1, b1, wqkv, bqkv, wd, bd, g2, b2, wi, bi, wo, bo, tables)
 
 
+PIECES = 4
+
+
 def a_index(b):
-    return jnp.where(b < 4, 0, jnp.where(b < 8, b - 3, jnp.where(b < 11, 5, 6)))
+    g = b // 4
+    return g * (2 - g) * (b - 3) + (g * (g - 1) // 2) * 5 + b // 11
 
 
 def b_index(b):
-    return jnp.where(b < 4, b, jnp.where(b < 8, 4, jnp.where(b < 11, b - 3, 4)))
-
-
-def weight_kernel(a_ref, b_ref, p_ref, nrm_ref):
-    n_mb, seq, d = a_ref.shape[1:]
-
-    @pl.when(pl.program_id(0) == 0)
+    g = b // 4
+    middle, late = g * (2 - g), g * (g - 1) // 2
+    return (1 - middle - late) * b + middle * 4 + late * (b - 3) - (b // 11) * 4
+
+
+def gradient_kernel(
+    nb,
+    a_hbm,
+    b_hbm,
+    small,
+    out_in,
+    out_out,
+    out_qkv,
+    out_dense,
+    out_vec,
+    out_nrm,
+    abuf,
+    bbuf,
+    own,
+    csend,
+    crecv,
+    fin,
+    yred,
+    leafy,
+    leafz,
+    midy,
+    midz,
+    yz,
+    vec,
+    vrecv,
+    nrm,
+    nrecv,
+    absem,
+    outsem,
+    s_core,
+    r_core,
+    s_yred,
+    r_yred,
+    s_leafy,
+    r_leafy,
+    s_leafz,
+    r_leafz,
+    s_midy,
+    r_midy,
+    s_midz,
+    r_midz,
+    s_yz,
+    r_yz,
+    s_toty,
+    r_toty,
+    s_boty,
+    r_boty,
+    s_totz,
+    r_totz,
+    s_lz,
+    r_lz,
+    s_ag,
+    r_ag,
+    s_vec,
+    r_vec,
+    s_nrm,
+    r_nrm,
+):
+    n_mb, seq, d = abuf.shape[1:]
+    pipe = lax.axis_index("pipe")
+    me = lax.axis_index("dp")
+    group, inner = me // 16, me % 16
+    z, y, core = inner // 4, (inner // 2) % 2, inner % 2
+    mid = (z // 2 + z % 2) == 1
+    leaf = jnp.logical_not(mid)
+
+    def at(z_, y_, core_):
+        return {"dp": group * 16 + (z_ * 2 + y_) * 2 + core_}
+
+    core_peer = at(z, y, 1 - core)
+    y_peer = at(z, 1 - y, core)
+    near = at(z + 1 - 2 * (z % 2), y, core)
+    across = at(3 - z, y, core)
+    pipe_peer = {"pipe": 1 - pipe}
+    zi = z // 2
+    y_mine, y_other = y, 1 - y
+    z_mine, z_other = 2 + zi, 3 - zi
+    half = core * PIECES
+
+    def remote(src, dst, send, recv, device):
+        return pltpu.make_async_remote_copy(
+            src_ref=src, dst_ref=dst, send_sem=send, recv_sem=recv, device_id=device, device_id_type=MESH
+        )
+
+    def c_core(b):
+        return remote(csend.at[b % 2], crecv.at[b], s_core.at[b % 2], r_core.at[b], core_peer)
+
+    def c_yred(b):
+        return remote(own.at[b, y_other], yred.at[b], s_yred.at[b], r_yred.at[b], y_peer)
+
+    def c_leafy(b):
+        return remote(own.at[b, y_mine], leafy.at[b], s_leafy.at[b], r_leafy.at[b], near)
+
+    def c_leafz(b):
+        return remote(own.at[b, pl.ds(2, 2)], leafz.at[b], s_leafz.at[b], r_leafz.at[b], near)
+
+    def c_midy(b):
+        return remote(own.at[b, y_mine], midy.at[b], s_midy.at[b], r_midy.at[b], across)
+
+    def c_midz(b):
+        return remote(own.at[b, z_other], midz.at[b], s_midz.at[b], r_midz.at[b], across)
+
+    def c_yz(b):
+        return remote(own.at[b, z_mine], yz.at[b], s_yz.at[b], r_yz.at[b], y_peer)
+
+    def piece(b, k):
+        return fin.at[b, half + k]
+
+    def c_toty(b):
+        return remote(piece(b, y_mine), piece(b, y_mine), s_toty.at[b], r_toty.at[b], near)
+
+    def c_boty(b):
+        return remote(piece(b, y_mine), piece(b, y_mine), s_boty.at[b], r_boty.at[b], y_peer)
+
+    def c_totz(b):
+        return remote(piece(b, z_mine), piece(b, z_mine), s_totz.at[b], r_totz.at[b], across)
+
+    def c_lz(b, which):
+        k = z_mine if which == 0 else z_other
+        return remote(piece(b, k), piece(b, k), s_lz.at[which, b], r_lz.at[which, b], near)
+
+    def c_ag(b, k):
+        return remote(piece(b, k), piece(b, k), s_ag.at[k, b], r_ag.at[k, b], core_peer)
+
+    vec_to = (core_peer, y_peer, near, across, near)
+
+    def c_vec(h):
+        return remote(vec.at[h], vrecv.at[h], s_vec.at[h], r_vec.at[h], vec_to[h])
+
+    def c_nrm():
+        return remote(nrm, nrecv, s_nrm, r_nrm, pipe_peer)
+
+    def c_load(b, which):
+        slot = b % 2
+        if which == 0:
+            return pltpu.make_async_copy(a_hbm.at[a_index(b)], abuf.at[slot], absem.at[0, slot])
+        return pltpu.make_async_copy(b_hbm.at[b_index(b)], bbuf.at[slot], absem.at[1, slot])
+
+    def add(*values):
+        total = values[0].astype(F32)
+        for v in values[1:]:
+            total = total + v.astype(F32)
+        return total
+
+    for which in range(2):
+        c_load(0, which).start()
+
+    barrier = pltpu.get_barrier_semaphore()
+    for device in (core_peer, y_peer, near, pipe_peer):
+        pl.semaphore_signal(barrier, inc=1, device_id=device, device_id_type=MESH)
+
+    @pl.when(mid)
     def _():
-        nrm_ref[...] = jnp.zeros_like(nrm_ref)
-
-    step = 256
-    for c in range(d // step):
-        cols = slice(c * step, (c + 1) * step)
-        total = None
-        for m in range(n_mb):
-            grad = dot_tn(a_ref[0, m], b_ref[0, m, :, cols])
-            squares = jnp.sum((grad * grad).reshape(d // 8, 8, step), axis=0)
-            nrm_ref[m] += squares[:, :128] + squares[:, 128:]
-            total = grad if total is None else total + grad
-        p_ref[0, :, cols] = total.astype(BF16)
-
-
-def weight_call(a, b):
+        pl.semaphore_signal(barrier, inc=1, device_id=across, device_id_type=MESH)
+        pl.semaphore_wait(barrier, 5)
+
+    @pl.when(leaf)
+    def _():
+        pl.semaphore_wait(barrier, 4)
+
+    row = lax.broadcasted_iota(jnp.int32, (16, d), 0)
+    total = None
+    for m in range(n_mb):
+        value = jnp.where(row < 12, small[m], 0.0)
+        squares = value * value * jnp.where(row == 7, 2.0, 1.0)
+        folded = squares[:8] + squares[8:]
+        nrm[m] = sum(folded[:, k * 128 : (k + 1) * 128] for k in range(d // 128))
+        total = value if total is None else total + value
+    vec[0] = total
+    c_vec(0).start()
+
+    def weight_block(b):
+        slot = b % 2
+        for which in range(2):
+            c_load(b, which).wait()
+
+        @pl.when(b + 1 < nb)
+        def _():
+            for which in range(2):
+                c_load(b + 1, which).start()
+
+        @pl.when(b >= 2)
+        def _():
+            c_core(b - 2).wait_send()
+
+        step = 256
+        for c in range(d // step):
+            cols = slice(c * step, (c + 1) * step)
+            total = None
+            for m in range(n_mb):
+                grad = dot_tn(abuf[slot, m], bbuf[slot, m, :, cols])
+                squares = jnp.sum((grad * grad).reshape(d // 8, 8, step), axis=0)
+                nrm[m] += squares[:, :128] + squares[:, 128:]
+                total = grad if total is None else total + grad
+            total = total.astype(BF16).reshape(2, PIECES, d // 8, step)
+
+            @pl.when(core == 0)
+            def _():
+                own[b, :, :, cols] = total[0]
+                csend[slot, :, :, cols] = total[1]
+
+            @pl.when(core == 1)
+            def _():
+                own[b, :, :, cols] = total[1]
+                csend[slot, :, :, cols] = total[0]
+
+        c_core(b).start()
+
+    def lag1(b):
+        c_core(b).wait_recv()
+        for k in range(PIECES):
+            own[b, k] = add(own[b, k], crecv[b, k]).astype(BF16)
+        c_yred(b).start()
+
+        @pl.when(leaf)
+        def _():
+            c_leafz(b).start()
+
+    def lag2(b):
+        @pl.when(mid)
+        def _():
+            c_leafz(b).wait_recv()
+            for k in range(2):
+                own[b, 2 + k] = add(own[b, 2 + k], leafz[b, k]).astype(BF16)
+            c_midz(b).start()
+
+        c_yred(b).wait_recv()
+        own[b, y_mine] = add(own[b, y_mine], yred[b]).astype(BF16)
+
+        @pl.when(leaf)
+        def _():
+            c_leafy(b).start()
+
+    def lag3(b):
+        @pl.when(mid)
+        def _():
+            c_midz(b).wait_recv()
+            own[b, z_mine] = add(own[b, z_mine], midz[b]).astype(BF16)
+            c_yz(b).start()
+            c_leafy(b).wait_recv()
+            own[b, y_mine] = add(own[b, y_mine], leafy[b]).astype(BF16)
+            c_midy(b).start()
+
+    def lag4(b):
+        @pl.when(mid)
+        def _():
+            c_yz(b).wait_recv()
+            fin[b, half + z_mine] = add(own[b, z_mine], yz[b]).astype(BF16)
+            c_totz(b).start()
+            c_lz(b, 0).start()
+            c_ag(b, z_mine).start()
+            c_midy(b).wait_recv()
+            fin[b, half + y_mine] = add(own[b, y_mine], midy[b]).astype(BF16)
+            c_toty(b).start()
+            c_boty(b).start()
+            c_ag(b, y_mine).start()
+
+    def lag5(b):
+        @pl.when(mid)
+        def _():
+            c_totz(b).wait_recv()
+            c_lz(b, 1).start()
+            c_ag(b, z_other).start()
+            c_boty(b).wait_recv()
+            c_ag(b, y_other).start()
+
+        @pl.when(leaf)
+        def _():
+            c_toty(b).wait_recv()
+            c_boty(b).start()
+            c_ag(b, y_mine).start()
+            c_lz(b, 0).wait_recv()
+            c_ag(b, z_mine).start()
+
+    def lag6(b):
+        @pl.when(leaf)
+        def _():
+            c_boty(b).wait_recv()
+            c_ag(b, y_other).start()
+            c_lz(b, 1).wait_recv()
+            c_ag(b, z_other).start()
+
+    def out_copies(b, act):
+        @pl.when(b // 4 == 0)
+        def _():
+            cols = pl.ds(pl.multiple_of(b * d, 128), d)
+            act(pltpu.make_async_copy(fin.at[b], out_in.at[:, :, cols], outsem.at[b]))
+
+        @pl.when(b // 4 == 1)
+        def _():
+            act(pltpu.make_async_copy(fin.at[b], out_out.at[b - 4], outsem.at[b]))
+
+        @pl.when((b // 4 == 2) & (b < 11))
+        def _():
+            cols = pl.ds(pl.multiple_of((b - 8) * d, 128), d)
+            act(pltpu.make_async_copy(fin.at[b], out_qkv.at[:, :, cols], outsem.at[b]))
+
+        @pl.when(b == 11)
+        def _():
+            act(pltpu.make_async_copy(fin.at[b], out_dense, outsem.at[b]))
+
+    def lag7(b):
+        for k in range(PIECES):
+            c_ag(b, k).wait_recv()
+        out_copies(b, lambda c: c.start())
+
+    def vector_steps(t):
+        @pl.when(t == 1)
+        def _():
+            c_vec(0).wait_recv()
+            vec[1] = vec[0] + vrecv[0]
+            c_vec(1).start()
+
+        @pl.when(t == 2)
+        def _():
+            c_vec(1).wait_recv()
+            vec[2] = vec[1] + vrecv[1]
+
+            @pl.when(leaf)
+            def _():
+                c_vec(2).start()
+
+        @pl.when((t == 3) & mid)
+        def _():
+            c_vec(2).wait_recv()
+            vec[3] = vec[2] + vrecv[2]
+            c_vec(3).start()
+
+        @pl.when((t == 4) & mid)
+        def _():
+            c_vec(3).wait_recv()
+            vec[4] = vec[3] + vrecv[3]
+            c_vec(4).start()
+            out_vec[...] = vec[4]
+
+        @pl.when((t == 5) & leaf)
+        def _():
+            c_vec(4).wait_recv()
+            out_vec[...] = vrecv[4]
+
+        @pl.when(t == nb)
+        def _():
+            c_nrm().start()
+
+    stages = (weight_block, lag1, lag2, lag3, lag4, lag5, lag6, lag7)
+
+    def step(t, carry):
+        for lag, stage in enumerate(stages):
+
+            @pl.when((t >= lag) & (t - lag < nb))
+            def _(lag=lag, stage=stage):
+                stage(t - lag)
+
+        vector_steps(t)
+        return carry
+
+    lax.fori_loop(0, nb + len(stages) - 1, step, 0)
+
+    c_nrm().wait_recv()
+    out_nrm[...] = nrm[...] + nrecv[...]
+    c_nrm().wait_send()
+    c_vec(0).wait_send()
+    c_vec(1).wait_send()
+    c_core(nb - 2).wait_send()
+    c_core(nb - 1).wait_send()
+
+    @pl.when(leaf)
+    def _():
+        c_vec(2).wait_send()
+
+    @pl.when(mid)
+    def _():
+        c_vec(3).wait_send()
+        c_vec(4).wait_send()
+
+    def drain(b, carry):
+        c_yred(b).wait_send()
+        c_boty(b).wait_send()
+        for k in range(PIECES):
+            c_ag(b, k).wait_send()
+
+        @pl.when(leaf)
+        def _():
+            c_leafy(b).wait_send()
+            c_leafz(b).wait_send()
+
+        @pl.when(mid)
+        def _():
+            c_midy(b).wait_send()
+            c_midz(b).wait_send()
+            c_yz(b).wait_send()
+            c_toty(b).wait_send()
+            c_totz(b).wait_send()
+            c_lz(b, 0).wait_send()
+            c_lz(b, 1).wait_send()
+
+        out_copies(b, lambda c: c.wait())
+        return carry
+
+    lax.fori_loop(0, nb, drain, 0)
+
+
+def gradient_call(a, b, small):
     n_mb, seq, d = a.shape[1:]
+    nb = 12
+    rows = d // 8
+    vmem = pl.BlockSpec(memory_space=pltpu.VMEM)
+    hbm = pl.BlockSpec(memory_space=pl.ANY)
+    dma = pltpu.SemaphoreType.DMA
+
+    def wide(columns):
+        return jax.ShapeDtypeStruct((8, rows, columns), BF16)
+
+    def slots(*lead):
+        return pltpu.VMEM(lead + (rows, d), BF16)
+
     return pl.pallas_call(
-        weight_kernel,
-        grid=(12,),
+        functools.partial(gradient_kernel, nb),
         out_shape=(
-            jax.ShapeDtypeStruct((12, d, d), BF16),
+            wide(4 * d),
+            jax.ShapeDtypeStruct((4, 8, rows, d), BF16),
+            wide(3 * d),
+            wide(d),
+            jax.ShapeDtypeStruct((16, d), F32),
             jax.ShapeDtypeStruct((n_mb, 8, 128), F32),
         ),
-        in_specs=[
-            pl.BlockSpec((1, n_mb, seq, d), lambda g: (a_index(g), 0, 0, 0)),
-            pl.BlockSpec((1, n_mb, seq, d), lambda g: (b_index(g), 0, 0, 0)),
-        ],
-        out_specs=(
-            pl.BlockSpec((1, d, d), lambda g: (g, 0, 0)),
-            pl.BlockSpec((n_mb, 8, 128), lambda g: (0, 0, 0)),
+        in_specs=[hbm, hbm, vmem],
+        out_specs=(hbm, hbm, hbm, hbm, vmem, vmem),
+        scratch_shapes=[
+            pltpu.VMEM((2, n_mb, seq, d), BF16),
+            pltpu.VMEM((2, n_mb, seq, d), BF16),
+            slots(nb, PIECES),
+            slots(2, PIECES),
+            slots(nb, PIECES),
+            slots(nb, 2 * PIECES),
+            slots(nb),
+            slots(nb),
+            slots(nb, 2),
+            slots(nb),
+            slots(nb),
+            slots(nb),
+            pltpu.VMEM((5, 16, d), F32),
+            pltpu.VMEM((5, 16, d), F32),
+            pltpu.VMEM((n_mb, 8, 128), F32),
+            pltpu.VMEM((n_mb, 8, 128), F32),
+            dma((2, 2)),
+            dma((nb,)),
+            dma((2,)),
+            dma((nb,)),
+        ]
+        + [dma((nb,)) for _ in range(18)]
+        + [dma((2, nb)), dma((2, nb)), dma((PIECES, nb)), dma((PIECES, nb)), dma((5,)), dma((5,)), dma, dma],
+        compiler_params=pltpu.CompilerParams(
+            collective_id=1, has_side_effects=True, vmem_limit_bytes=62 * 2**20
         ),
-        compiler_params=pltpu.CompilerParams(vmem_limit_bytes=48 * 2**20),
         cost_estimate=pl.CostEstimate(
-            flops=12 * 2 * n_mb * seq * d * d, bytes_accessed=40 * 2**20, transcendentals=0
+            flops=nb * 2 * n_mb * seq * d * d, bytes_accessed=64 * 2**20, transcendentals=0
         ),
-    )(a, b)
-
-
-def on_device(inputs, cotangent, lengths, *params):
+    )(a, b, small)
+
+
+def on_device(size, inputs, cotangent, lengths, *params):
     n_mb, seq, d = inputs.shape
     tables = jnp.asarray(rotary_tables(seq))
     out_y, out_dx, a, b, small = section_call(lengths, inputs, cotangent, params, tables)
-    partial, nrm = weight_call(a, b)
-    small = small[:, :12]
-    weight = jnp.ones((12, 1), F32).at[7].set(2.0)
-    norms = jnp.sum(nrm, axis=(1, 2)) + jnp.sum(small * small * weight, axis=(1, 2))
-    norms = lax.psum(norms, "pipe")
-    summed = lax.psum(partial, "dp").astype(F32)
-    vectors = lax.psum(jnp.sum(small, axis=0), "dp")
+    w_in, w_out, w_qkv, w_dense, vectors, nrm = gradient_call(a, b, small)
+    sums = [w_in, w_out, w_qkv, w_dense, vectors]
+    if size > 16:
+        groups = [[g * 16 + r for g in range(size // 16)] for r in range(16)]
+        sums = [lax.psum(v, "dp", axis_index_groups=groups) for v in sums]
+    w_in, w_out, w_qkv, w_dense, vectors = [v.astype(F32) for v in sums]
+    norms = jnp.sum(nrm, axis=(1, 2))
     rows = [vectors[k : k + 1] for k in range(12)]
-    w_in = jnp.concatenate([summed[k] for k in range(4)], axis=1)[None]
-    w_out = summed[4:8].reshape(1, 4 * d, d)
-    w_qkv = jnp.concatenate([summed[8 + k] for k in range(3)], axis=1)[None]
-    w_dense = summed[11:12]
     return (
         out_y,
         out_dx,
         rows[0],
         rows[1],
-        w_qkv,
+        w_qkv.reshape(1, d, 3 * d),
         vectors[4:7].reshape(1, 3 * d),
-        w_dense,
+        w_dense.reshape(1, d, d),
         rows[7],
         rows[2],
         rows[3],
-        w_in,
+        w_in.reshape(1, d, 4 * d),
         vectors[8:12].reshape(1, 4 * d),
-        w_out,
+        w_out.reshape(1, 4 * d, d),
         rows[7],
         norms,
     )
@@ -487,7 +907,7 @@
     weights = (vector, vector, matrix, vector, matrix, vector) * 2
     tokens = P("dp", None, None)
     return jax.shard_map(
-        on_device,
+        functools.partial(on_device, mesh.shape["dp"]),
         mesh=mesh,
         in_specs=(tokens, tokens, P("dp")) + weights,
         out_specs=(P("pipe", "dp", None, None),) * 2 + weights + (P("dp"),),

time: 472 us -> 320 us (0.68)
  waiting for transfers between devices: 187 us -> 0 us
  Pallas kernels: 157 us -> 293 us
  blocking collectives: 68.4 us -> 0 us
  between operations: 14.1 us -> 0.69 us
  local copies, waits for them, and re-layouts: 20.4 us -> 7.53 us
  other arithmetic: 24.9 us -> 18 us
    psum x1 -> x0, waiting for transfers between devices: 187 us -> none  [on_device(): summed = lax.psum(partial, 'dp').astype(F32)]
    pallas_call x1, Pallas kernels: 24 us -> 160 us  [gradient_call(): pl.pallas_call(functools.partial(gradient_kernel, nb), out_shape=(wide(4...]
    psum x2 -> x0, blocking collectives: 68.4 us -> none  [the longest x1 62.9 us: on_device(): vectors = lax.psum(jnp.sum(small, axis=0), 'dp')]
    reshape x0 -> x4, other arithmetic: none -> 16.5 us  [the longest x1 5.05 us: on_device(): w_in.reshape(1, d, 4 * d)]
    convert_element_type x1 -> x0, other arithmetic: 15.7 us -> none  [on_device(): summed = lax.psum(partial, 'dp').astype(F32)]
    broadcast_in_dim x2 -> x0, other arithmetic: 8.91 us -> none  [the longest x1 5.07 us: on_device(): w_in = jnp.concatenate([summed[k] for k in range(4)], axis=1)[None]]
    squeeze x1 -> x0, local copies, waits for them, and re-layouts: 6.55 us -> none  [on_device(): w_in = jnp.concatenate([summed[k] for k in range(4)], axis=1)[None]]
    slice x2 -> x0, local copies, waits for them, and re-layouts: 6.14 us -> none  [the longest x1 4.56 us: on_device(): w_out = summed[4:8].reshape(1, 4 * d, d)]
  transfers between devices with their start and end apart: 1 -> 0, of which waited for: 1 -> 0; matrix products, arithmetic and copies ran while one was open for 0% -> 0% of each run, Pallas kernels for 0% -> 0%
where the time goes in v2:
time: 320 us; the launch traced here: 319 us
  Pallas kernels  293 us (92%)
  other arithmetic  18 us (6%)
  local copies, waits for them, and re-layouts  7.53 us (2%)
    pallas_call x1, Pallas kernels, gradient_call(): pl.pallas_call(functools.partial(gradient_kernel, nb), out_shape=(wide(4...  160 us
    pallas_call x1, Pallas kernels, section_call(): pl.pallas_call(functools.partial(section_kernel, n_mb), out_shape=(jax.Sh...  133 us

profile of v2, /device:TPU:0, one launch (start us, length us, event | category | flops | bytes accessed | tf_op | source)
XLA Modules:
  0.0 319.2 jit_solution(2920388230504886043)
XLA Ops:
  0.7 133.2 %shard_map.271 = (bf16[1,4,256,768]{3,2,1,0:T(8,128)(2,1)}, bf16[1,4,256,768]{3,2,1,0:T(8,128)(2,1)}, bf16[7,4,256,768]{3,2,1,0:T(8,128)(2,1)}, bf16[8,4,256,768]{3,2,1,0:T(8,128)(2,1)}, f32[4,16,768]{2,1,0:T(8,128)}) custom-call(s32[4]{0:T(128)} %lens.1, bf16[4,256,768]{2,1,0:T(8,128)(2,1)} %inputs.1, bf16[4,256,768]{2,1,0:T(8,128)(2,1)} %cot.1, ...), custom_call_target="tpu_custom_call" | custom-call | flops 28991029248 | bytes 41943040 | tf_op jit(solution)/shard_map/pallas_call | solution.py:355
  133.9 159.8 %shard_map.272 = (bf16[8,96,3072]{2,1,0:T(8,128)(2,1)}, bf16[4,8,96,768]{3,2,1,0:T(8,128)(2,1)}, bf16[8,96,2304]{2,1,0:T(8,128)(2,1)}, bf16[8,96,768]{2,1,0:T(8,...) custom-call(bf16[7,4,256,768]{3,2,1,0:T(8,128)(2,1)} %get-tuple-element.28.a_hbm, ...), custom_call_target="tpu_custom_call" | custom-call | flops 14495514624 | bytes 67108864 | tf_op jit(solution)/shard_map/pallas_call | solution.py:829
  293.6 0.0 copy-start.1
  293.6 1.5 reduce_sum.9
  295.1 0.7 slice_bitcast_fusion.1
  295.9 0.6 copy.31
  296.5 0.7 slice_bitcast_fusion
  297.2 1.5 fusion
  298.7 0.0 copy-start.4
  298.7 0.6 copy.32
  299.4 2.8 bitcast_convert_fusion.2
  302.2 0.0 copy-done.1
  302.2 0.0 copy-start
  302.2 0.0 slice-start
  302.2 4.1 %bitcast_convert_fusion.1 = f32[1,768,2304]{2,1,0:T(8,128)} fusion(bf16[1,768,2304]{2,1,0:T(8,128)(2,1)S(1)} %bitcast.26), kind=kLoop, calls=%fused_computation.1 | loop fusion | flops 1769472 | bytes 10616832 | tf_op jit(solution)/shard_map/reshape | solution.py:891
  306.3 0.4 copy-done
  306.7 0.0 slice-start.1
  306.7 5.0 %bitcast_convert_fusion = f32[1,768,3072]{2,1,0:T(8,128)} fusion(bf16[1,768,3072]{2,1,0:T(8,128)(2,1)S(1)} %bitcast.25), kind=kLoop, calls=%fused_computation | loop fusion | flops 2359296 | bytes 14155776 | tf_op jit(solution)/shard_map/reshape | solution.py:897
  311.8 0.0 slice-done
  311.8 0.0 slice-done.1
  311.8 0.0 copy-start.3
  311.8 4.5 %convert.7 = f32[1,3072,768]{2,1,0:T(8,128)} convert(bf16[1,3072,768]{2,1,0:T(8,128)(2,1)S(1)} %bitcast.24) | non-fusion elementwise | flops 2359296 | bytes 14155776 | tf_op jit(solution)/shard_map/reshape | solution.py:899
  316.3 0.0 copy-done.4
  316.3 0.0 copy-start.2
  316.3 0.6 copy.36
  316.9 0.0 copy-done.3
  316.9 1.1 copy.37
  318.0 0.0 copy-done.2
  318.0 1.1 copy.38
  (1 shorter events, 0.0 us)
Async XLA Ops:
  293.6 8.6 %copy-start.1 = (bf16[8,96,2304]{2,1,0:T(8,128)(2,1)S(1)}, bf16[8,96,2304]{2,1,0:T(8,128)(2,1)}, u32[]{:S(2)}) copy-start(bf16[8,96,2304]{2,1,0:T(8,128)(2,1)} %get-tuple-element.32) | copy-start | bytes 10616836
  298.7 17.5 %copy-start.4 = (f32[1,768]{1,0:T(1,128)}, f32[1,768]{1,0:T(1,128)S(1)}, u32[]{:S(2)}) copy-start(f32[1,768]{1,0:T(1,128)S(1)} %get-tuple-element.94) | copy-start | bytes 9220
  302.2 4.5 %copy-start = (bf16[8,96,3072]{2,1,0:T(8,128)(2,1)S(1)}, bf16[8,96,3072]{2,1,0:T(8,128)(2,1)}, u32[]{:S(2)}) copy-start(bf16[8,96,3072]{2,1,0:T(8,128)(2,1)} %get-tuple-element.34) | copy-start | bytes 14155780
  302.2 9.6 %slice-start = ((s8[4718592]{0:T(1024)(128)(4,1)}), s8[4194304]{0:T(1024)(128)(4,1)S(1)}, s32[]{:S(2)}) async-start(s8[4718592]{0:T(1024)(128)(4,1)} %bitcast.22), calls=%async_computation | async-start | bytes 8388608
  306.7 5.1 %slice-start.1 = ((s8[4718592]{0:T(1024)(128)(4,1)}), s8[524288]{0:T(1024)(128)(4,1)S(1)}, s32[]{:S(2)}) async-start(s8[4718592]{0:T(1024)(128)(4,1)} %bitcast.22), calls=%async_computation.1 | async-start | bytes 1048576
  311.8 5.1 %copy-start.3 = (bf16[1,4,256,768]{3,2,1,0:T(8,128)(2,1)S(1)}, bf16[1,4,256,768]{3,2,1,0:T(8,128)(2,1)}, u32[]{:S(2)}) copy-start(bf16[1,4,256,768]{3,2,1,0:T(8,128)(2,1)} %get-tuple-element.87) | copy-start | bytes 4718596
  316.3 1.7 copy-start.2

commit v3 on v2

--- a/solution.py
+++ b/solution.py
@@ -161,7 +161,13 @@
         inverse = lax.rsqrt(jnp.mean(center * center, axis=-1, keepdims=True) + EPSILON)
         return x, center * inverse, inverse
 
-    def forward(i, carry):
+    def both_parts(attend, feed):
+        for k in range(pairs):
+            attend(k)
+        for k in range(4):
+            feed(k)
+
+    def forward(i):
         @pl.when(last)
         def _():
             fcopy(i).wait_recv()
@@ -176,7 +182,7 @@
         def _():
             wcopies[0].wait()
 
-        for t in range(3):
+        for t in (2, 1, 0):
             mixed = dot_nn(a1, wqkv_v[:, t * d : (t + 1) * d]) + bqkv[:, t * d : (t + 1) * d]
             if t == 2:
                 bv[5 + t, i] = mixed.astype(BF16)
@@ -191,8 +197,8 @@
         query = lax.broadcasted_iota(jnp.int32, (seq, seq), 1)
         bias_v[...] = jnp.where((key <= query) & (key < lens[i]), 0.0, NEG_FILL)
 
-        def attend(hp, carry):
-            cols = pl.ds(pl.multiple_of(hp * 128, 128), 128)
+        def attend(hp):
+            cols = slice(hp * 128, (hp + 1) * 128)
             qp, kp, vp = bv[5, i, :, cols], bv[6, i, :, cols], bv[7, i, :, cols]
             ctx = None
             for a in range(2):
@@ -203,29 +209,25 @@
                 part = dot_tn(probs, pick(vp, a))
                 ctx = part if ctx is None else ctx + part
             av[6, i, :, cols] = ctx.astype(BF16)
-            return carry
-
-        lax.fori_loop(0, pairs, attend, 0)
 
         @pl.when(i == 0)
         def _():
             for k in (1, 2, 3):
                 wcopies[k].wait()
 
-        acc[...] = x + dot_nn(av[6, i], wd_v[...]) + bd[...] + bo[...]
-
-        def feed(j, carry):
-            cols = pl.ds(pl.multiple_of(j * d, 128), d)
+        acc[...] = xb[i].astype(F32) + bd[...] + bo[...]
+
+        def feed(j):
+            cols = slice(j * d, (j + 1) * d)
             hidden = dot_nn(av[0, i], wi_v[:, cols]) + bi[:, cols]
             gate = 0.5 * (1.0 + lax.erf(hidden * INV_ROOT_TWO))
             act = (hidden * gate).astype(BF16)
             av[1 + j, i] = act
             bv[j, i] = (gate + hidden * jnp.exp(-0.5 * hidden * hidden) * INV_ROOT_TWO_PI).astype(BF16)
-            acc[...] += dot_nn(act, wo_v[pl.ds(pl.multiple_of(j * d, 128), d), :])
-            return carry
-
-        lax.fori_loop(0, 4, feed, 0)
-        yb[i] = acc[...].astype(BF16)
+            acc[...] += dot_nn(act, wo_v[j * d : (j + 1) * d, :])
+
+        both_parts(attend, feed)
+        yb[i] = (acc[...] + dot_nn(av[6, i], wd_v[...])).astype(BF16)
 
         @pl.when(first)
         def _():
@@ -234,9 +236,8 @@
         pltpu.make_async_copy(yb.at[i], out_y.at[0, i], ysem.at[i]).start()
         for k in range(7):
             pltpu.make_async_copy(av.at[k, i], a_hbm.at[k, i], asem.at[k, i]).start()
-        return carry
-
-    def backward(i, carry):
+
+    def backward(i):
         @pl.when(first)
         def _():
             bcopy(i).wait_recv()
@@ -251,20 +252,18 @@
         small[i, 7:8, :] = jnp.sum(gy.astype(F32), axis=0, keepdims=True)
         acc[...] = jnp.zeros_like(acc)
 
-        def feed(j, carry):
-            cols = pl.ds(pl.multiple_of(j * d, 128), d)
-            dact = dot_nt(bv[4, i], wo_v[pl.ds(pl.multiple_of(j * d, 128), d), :])
+        def feed(j):
+            cols = slice(j * d, (j + 1) * d)
+            dact = dot_nt(bv[4, i], wo_v[j * d : (j + 1) * d, :])
             dh = (dact * bv[j, i].astype(F32)).astype(BF16)
             bv[j, i] = dh
-            small[i, pl.ds(8 + j, 1), :] = jnp.sum(dh.astype(F32), axis=0, keepdims=True)
+            small[i, 8 + j : 9 + j, :] = jnp.sum(dh.astype(F32), axis=0, keepdims=True)
             acc[...] += dot_nt(dh, wi_v[:, cols])
-            return carry
-
-        lax.fori_loop(0, 4, feed, 0)
+
         dctx_v[...] = dot_nt(gy, wd_v[...]).astype(BF16)
 
-        def attend(hp, carry):
-            cols = pl.ds(pl.multiple_of(hp * 128, 128), 128)
+        def attend(hp):
+            cols = slice(hp * 128, (hp + 1) * 128)
             qp, kp, vp = bv[5, i, :, cols], bv[6, i, :, cols], bv[7, i, :, cols]
             dop = dctx_v[:, cols]
             dq = dk = dv = None
@@ -284,9 +283,8 @@
                 w = w.astype(BF16)
                 bv[5 + t, i, :, cols] = w
                 small[i, 4 + t : 5 + t, cols] = jnp.sum(w.astype(F32), axis=0, keepdims=True)
-            return carry
-
-        lax.fori_loop(0, pairs, attend, 0)
+
+        both_parts(attend, feed)
         da1 = dot_nt(bv[5, i], wqkv_v[:, 0:d])
         da1 = da1 + dot_nt(bv[6, i], wqkv_v[:, d : 2 * d])
         da1 = da1 + dot_nt(bv[7, i], wqkv_v[:, 2 * d : 3 * d])
@@ -309,19 +307,30 @@
         pltpu.make_async_copy(dxb.at[i], out_dx.at[0, i], dxsem.at[i]).start()
         for k in range(8):
             pltpu.make_async_copy(bv.at[k, i], b_hbm.at[k, i], bsem.at[k, i]).start()
-        return carry
 
     @pl.when(first)
     def _():
         pltpu.make_async_copy(inputs, xb, insem).wait()
 
-    lax.fori_loop(0, n_mb, forward, 0)
-
     @pl.when(last)
     def _():
         pltpu.make_async_copy(cot, bv.at[4], cotsem).wait()
 
-    lax.fori_loop(0, n_mb, backward, 0)
+    def tick(step, carry):
+        phase = section * (step % 2) + (1 - section) * (step // n_mb)
+        mb = section * (step // 2) + (1 - section) * (step % n_mb)
+
+        @pl.when(phase == 0)
+        def _():
+            forward(mb)
+
+        @pl.when(phase == 1)
+        def _():
+            backward(mb)
+
+        return carry
+
+    lax.fori_loop(0, 2 * n_mb, tick, 0)
 
     def drain(i, carry):
         @pl.when(first)
@@ -397,6 +406,7 @@
 
 
 PIECES = 4
+SPLITS = 2
 
 
 def a_index(b):
@@ -542,11 +552,11 @@
     def c_nrm():
         return remote(nrm, nrecv, s_nrm, r_nrm, pipe_peer)
 
-    def c_load(b, which):
-        slot = b % 2
+    def c_load(w, which):
+        slot = w % 2
         if which == 0:
-            return pltpu.make_async_copy(a_hbm.at[a_index(b)], abuf.at[slot], absem.at[0, slot])
-        return pltpu.make_async_copy(b_hbm.at[b_index(b)], bbuf.at[slot], absem.at[1, slot])
+            return pltpu.make_async_copy(a_hbm.at[a_index(w)], abuf.at[slot], absem.at[0, slot])
+        return pltpu.make_async_copy(b_hbm.at[b_index(w)], bbuf.at[slot], absem.at[1, slot])
 
     def add(*values):
         total = values[0].astype(F32)
@@ -583,28 +593,34 @@
 
     def weight_block(b):
         slot = b % 2
-        for which in range(2):
-            c_load(b, which).wait()
-
-        @pl.when(b + 1 < nb)
+        w, part = b // SPLITS, b % SPLITS
+        wslot = w % 2
+
+        @pl.when(part == 0)
         def _():
             for which in range(2):
-                c_load(b + 1, which).start()
+                c_load(w, which).wait()
+
+        @pl.when((part == 0) & (w + 1 < nb // SPLITS))
+        def _():
+            for which in range(2):
+                c_load(w + 1, which).start()
 
         @pl.when(b >= 2)
         def _():
             c_core(b - 2).wait_send()
 
         step = 256
+        lhs = pl.ds(pl.multiple_of(part * (d // SPLITS), 128), d // SPLITS)
         for c in range(d // step):
             cols = slice(c * step, (c + 1) * step)
             total = None
             for m in range(n_mb):
-                grad = dot_tn(abuf[slot, m], bbuf[slot, m, :, cols])
-                squares = jnp.sum((grad * grad).reshape(d // 8, 8, step), axis=0)
+                grad = dot_tn(abuf[wslot, m, :, lhs], bbuf[wslot, m, :, cols])
+                squares = jnp.sum((grad * grad).reshape(-1, 8, step), axis=0)
                 nrm[m] += squares[:, :128] + squares[:, 128:]
                 total = grad if total is None else total + grad
-            total = total.astype(BF16).reshape(2, PIECES, d // 8, step)
+            total = total.astype(BF16).reshape(2, PIECES, -1, step)
 
             @pl.when(core == 0)
             def _():
@@ -693,23 +709,26 @@
             c_ag(b, z_other).start()
 
     def out_copies(b, act):
-        @pl.when(b // 4 == 0)
-        def _():
-            cols = pl.ds(pl.multiple_of(b * d, 128), d)
-            act(pltpu.make_async_copy(fin.at[b], out_in.at[:, :, cols], outsem.at[b]))
-
-        @pl.when(b // 4 == 1)
-        def _():
-            act(pltpu.make_async_copy(fin.at[b], out_out.at[b - 4], outsem.at[b]))
-
-        @pl.when((b // 4 == 2) & (b < 11))
-        def _():
-            cols = pl.ds(pl.multiple_of((b - 8) * d, 128), d)
-            act(pltpu.make_async_copy(fin.at[b], out_qkv.at[:, :, cols], outsem.at[b]))
-
-        @pl.when(b == 11)
-        def _():
-            act(pltpu.make_async_copy(fin.at[b], out_dense, outsem.at[b]))
+        w = b // SPLITS
+        rows = pl.ds((b % SPLITS) * 2 * PIECES, 2 * PIECES)
+
+        @pl.when(w // 4 == 0)
+        def _():
+            cols = pl.ds(pl.multiple_of(w * d, 128), d)
+            act(pltpu.make_async_copy(fin.at[b], out_in.at[rows, :, cols], outsem.at[b]))
+
+        @pl.when(w // 4 == 1)
+        def _():
+            act(pltpu.make_async_copy(fin.at[b], out_out.at[w - 4, rows], outsem.at[b]))
+
+        @pl.when((w // 4 == 2) & (w < 11))
+        def _():
+            cols = pl.ds(pl.multiple_of((w - 8) * d, 128), d)
+            act(pltpu.make_async_copy(fin.at[b], out_qkv.at[rows, :, cols], outsem.at[b]))
+
+        @pl.when(w == 11)
+        def _():
+            act(pltpu.make_async_copy(fin.at[b], out_dense.at[rows], outsem.at[b]))
 
     def lag7(b):
         for k in range(PIECES):
@@ -814,14 +833,15 @@
 
 def gradient_call(a, b, small):
     n_mb, seq, d = a.shape[1:]
-    nb = 12
-    rows = d // 8
+    nb = 12 * SPLITS
+    lead = 2 * PIECES * SPLITS
+    rows = d // lead
     vmem = pl.BlockSpec(memory_space=pltpu.VMEM)
     hbm = pl.BlockSpec(memory_space=pl.ANY)
     dma = pltpu.SemaphoreType.DMA
 
     def wide(columns):
-        return jax.ShapeDtypeStruct((8, rows, columns), BF16)
+        return jax.ShapeDtypeStruct((lead, rows, columns), BF16)
 
     def slots(*lead):
         return pltpu.VMEM(lead + (rows, d), BF16)
@@ -830,7 +850,7 @@
         functools.partial(gradient_kernel, nb),
         out_shape=(
             wide(4 * d),
-            jax.ShapeDtypeStruct((4, 8, rows, d), BF16),
+            jax.ShapeDtypeStruct((4, lead, rows, d), BF16),
             wide(3 * d),
             wide(d),
             jax.ShapeDtypeStruct((16, d), F32),
@@ -866,7 +886,7 @@
             collective_id=1, has_side_effects=True, vmem_limit_bytes=62 * 2**20
         ),
         cost_estimate=pl.CostEstimate(
-            flops=nb * 2 * n_mb * seq * d * d, bytes_accessed=64 * 2**20, transcendentals=0
+            flops=24 * n_mb * seq * d * d, bytes_accessed=64 * 2**20, transcendentals=0
         ),
     )(a, b, small)
 

time: 320 us -> 286 us (0.89)
  Pallas kernels: 293 us -> 259 us
    pallas_call x1, Pallas kernels: 133 us -> 106 us  [section_call(): pl.pallas_call(functools.partial(section_kernel, n_mb), out_shape=(jax.Sh...]
    pallas_call x1, Pallas kernels: 160 us -> 152 us  [gradient_call(): pl.pallas_call(functools.partial(gradient_kernel, nb), out_shape=(wide(4...]
where the time goes in v3:
time: 286 us; the launch traced here: 285 us
  Pallas kernels  259 us (91%)
  other arithmetic  18 us (6%)
  local copies, waits for them, and re-layouts  7.53 us (3%)
    pallas_call x1, Pallas kernels, gradient_call(): pl.pallas_call(functools.partial(gradient_kernel, nb), out_shape=(wide(4...  152 us
    pallas_call x1, Pallas kernels, section_call(): pl.pallas_call(functools.partial(section_kernel, n_mb), out_shape=(jax.Sh...  106 us
    unnamed x21, local copies, waits for them, and re-layouts  6.02 us

profile of v3, /device:TPU:0, one launch (start us, length us, event | category | flops | bytes accessed | tf_op | source)
XLA Modules:
  0.0 284.9 jit_solution(13778302676475852303)
XLA Ops:
  0.7 106.5 %shard_map.271 = (bf16[1,4,256,768]{3,2,1,0:T(8,128)(2,1)}, bf16[1,4,256,768]{3,2,1,0:T(8,128)(2,1)}, bf16[7,4,256,768]{3,2,1,0:T(8,128)(2,1)}, bf16[8,4,256,768]{3,2,1,0:T(8,128)(2,1)}, f32[4,16,768]{2,1,0:T(8,128)}) custom-call(s32[4]{0:T(128)} %lens.1, bf16[4,256,768]{2,1,0:T(8,128)(2,1)} %inputs.1, bf16[4,256,768]{2,1,0:T(8,128)(2,1)} %cot.1, ...), custom_call_target="tpu_custom_call" | custom-call | flops 28991029248 | bytes 41943040 | tf_op jit(solution)/shard_map/pallas_call | solution.py:364
  107.2 152.3 %shard_map.272 = (bf16[16,48,3072]{2,1,0:T(8,128)(2,1)}, bf16[4,16,48,768]{3,2,1,0:T(8,128)(2,1)}, bf16[16,48,2304]{2,1,0:T(8,128)(2,1)}, bf16[16,48,768]{2,1,0:...) custom-call(bf16[7,4,256,768]{3,2,1,0:T(8,128)(2,1)} %get-tuple-element.28.a_hbm, ...), custom_call_target="tpu_custom_call" | custom-call | flops 14495514624 | bytes 67108864 | tf_op jit(solution)/shard_map/pallas_call | solution.py:849
  259.4 0.0 copy-start.1
  259.4 1.5 reduce_sum.9
  260.9 0.7 slice_bitcast_fusion.1
  261.7 0.6 copy.31
  262.3 0.7 slice_bitcast_fusion
  263.0 1.5 fusion
  264.5 0.0 copy-start.4
  264.5 0.6 copy.32
  265.1 2.8 bitcast_convert_fusion.2
  268.0 0.0 copy-done.1
  268.0 0.0 copy-start
  268.0 0.0 slice-start
  268.0 4.1 %bitcast_convert_fusion.1 = f32[1,768,2304]{2,1,0:T(8,128)} fusion(bf16[1,768,2304]{2,1,0:T(8,128)(2,1)S(1)} %bitcast.26), kind=kLoop, calls=%fused_computation.1 | loop fusion | flops 1769472 | bytes 10616832 | tf_op jit(solution)/shard_map/reshape | solution.py:911
  272.1 0.4 copy-done
  272.5 0.0 slice-start.1
  272.5 5.0 %bitcast_convert_fusion = f32[1,768,3072]{2,1,0:T(8,128)} fusion(bf16[1,768,3072]{2,1,0:T(8,128)(2,1)S(1)} %bitcast.25), kind=kLoop, calls=%fused_computation | loop fusion | flops 2359296 | bytes 14155776 | tf_op jit(solution)/shard_map/reshape | solution.py:917
  277.6 0.0 slice-done
  277.6 0.0 slice-done.1
  277.6 0.0 copy-start.3
  277.6 4.5 %convert.7 = f32[1,3072,768]{2,1,0:T(8,128)} convert(bf16[1,3072,768]{2,1,0:T(8,128)(2,1)S(1)} %bitcast.24) | non-fusion elementwise | flops 2359296 | bytes 14155776 | tf_op jit(solution)/shard_map/reshape | solution.py:919
  282.1 0.0 copy-done.4
  282.1 0.0 copy-start.2
  282.1 0.6 copy.36
  282.7 0.0 copy-done.3
  282.7 1.1 copy.37
  283.8 0.0 copy-done.2
  283.8 1.1 copy.38
  (1 shorter events, 0.0 us)
Async XLA Ops:
  259.4 8.6 %copy-start.1 = (bf16[16,48,2304]{2,1,0:T(8,128)(2,1)S(1)}, bf16[16,48,2304]{2,1,0:T(8,128)(2,1)}, u32[]{:S(2)}) copy-start(bf16[16,48,2304]{2,1,0:T(8,128)(2,1)} %get-tuple-element.32) | copy-start | bytes 10616836
  264.5 17.5 %copy-start.4 = (f32[1,768]{1,0:T(1,128)}, f32[1,768]{1,0:T(1,128)S(1)}, u32[]{:S(2)}) copy-start(f32[1,768]{1,0:T(1,128)S(1)} %get-tuple-element.94) | copy-start | bytes 9220
  268.0 4.5 %copy-start = (bf16[16,48,3072]{2,1,0:T(8,128)(2,1)S(1)}, bf16[16,48,3072]{2,1,0:T(8,128)(2,1)}, u32[]{:S(2)}) copy-start(bf16[16,48,3072]{2,1,0:T(8,128)(2,1)} %get-tuple-element.34) | copy-start | bytes 14155780
  268.0 9.6 %slice-start = ((s8[4718592]{0:T(1024)(128)(4,1)}), s8[4194304]{0:T(1024)(128)(4,1)S(1)}, s32[]{:S(2)}) async-start(s8[4718592]{0:T(1024)(128)(4,1)} %bitcast.22), calls=%async_computation | async-start | bytes 8388608
  272.5 5.1 %slice-start.1 = ((s8[4718592]{0:T(1024)(128)(4,1)}), s8[524288]{0:T(1024)(128)(4,1)S(1)}, s32[]{:S(2)}) async-start(s8[4718592]{0:T(1024)(128)(4,1)} %bitcast.22), calls=%async_computation.1 | async-start | bytes 1048576
  277.6 5.1 %copy-start.3 = (bf16[1,4,256,768]{3,2,1,0:T(8,128)(2,1)S(1)}, bf16[1,4,256,768]{3,2,1,0:T(8,128)(2,1)}, u32[]{:S(2)}) copy-start(bf16[1,4,256,768]{3,2,1,0:T(8,128)(2,1)} %get-tuple-element.87) | copy-start | bytes 4718596
  282.1 1.7 copy-start.2

commit v4 on v3

--- a/solution.py
+++ b/solution.py
@@ -161,11 +161,26 @@
         inverse = lax.rsqrt(jnp.mean(center * center, axis=-1, keepdims=True) + EPSILON)
         return x, center * inverse, inverse
 
-    def both_parts(attend, feed):
-        for k in range(pairs):
-            attend(k)
-        for k in range(4):
-            feed(k)
+    def pair_columns(h):
+        return slice((h // 2) * 128, (h // 2 + 1) * 128)
+
+    def pipelined(stages, count, extra):
+        for t in range(count + max(lag for lag, _ in stages)):
+            for run in extra.get(t, ()):
+                run()
+            for lag, stage in stages:
+                if 0 <= t - lag < count:
+                    stage(t - lag)
+
+    def feed_slots(feed_in, feed_mid, feed_out):
+        slots = {}
+        for k in range(6):
+            runs = []
+            for lag, stage in ((2, feed_out), (1, feed_mid), (0, feed_in)):
+                if 0 <= k - lag < 4:
+                    runs.append(functools.partial(stage, k - lag))
+            slots[(5 * k) // 2] = runs
+        return slots
 
     def forward(i):
         @pl.when(last)
@@ -182,51 +197,68 @@
         def _():
             wcopies[0].wait()
 
-        for t in (2, 1, 0):
-            mixed = dot_nn(a1, wqkv_v[:, t * d : (t + 1) * d]) + bqkv[:, t * d : (t + 1) * d]
+        mixed = {}
+
+        def project(t):
+            mixed[t] = dot_nn(a1, wqkv_v[:, t * d : (t + 1) * d]) + bqkv[:, t * d : (t + 1) * d]
+
+        def settle(t):
             if t == 2:
-                bv[5 + t, i] = mixed.astype(BF16)
-            else:
-                for hp in range(pairs):
-                    w = rotate(mixed[:, hp * 128 : (hp + 1) * 128], 1.0)
-                    if t == 0:
-                        w = w * HEAD ** (-0.5)
-                    bv[5 + t, i, :, hp * 128 : (hp + 1) * 128] = w.astype(BF16)
-
+                bv[7, i] = mixed[2].astype(BF16)
+                return
+            for hp in range(pairs):
+                w = rotate(mixed[t][:, hp * 128 : (hp + 1) * 128], 1.0)
+                if t == 0:
+                    w = w * HEAD ** (-0.5)
+                bv[5 + t, i, :, hp * 128 : (hp + 1) * 128] = w.astype(BF16)
+
+        pipelined(((0, project), (1, settle)), 3, {})
         key = lax.broadcasted_iota(jnp.int32, (seq, seq), 0)
         query = lax.broadcasted_iota(jnp.int32, (seq, seq), 1)
         bias_v[...] = jnp.where((key <= query) & (key < lens[i]), 0.0, NEG_FILL)
 
-        def attend(hp):
-            cols = slice(hp * 128, (hp + 1) * 128)
-            qp, kp, vp = bv[5, i, :, cols], bv[6, i, :, cols], bv[7, i, :, cols]
-            ctx = None
-            for a in range(2):
-                scores = dot_nt(pick(kp, a), qp) + bias_v[...]
-                expo = jnp.exp(scores - jnp.max(scores, axis=0, keepdims=True))
-                probs = (expo * (1.0 / jnp.sum(expo, axis=0, keepdims=True))).astype(BF16)
-                pb[i, 2 * hp + a] = probs
-                part = dot_tn(probs, pick(vp, a))
-                ctx = part if ctx is None else ctx + part
-            av[6, i, :, cols] = ctx.astype(BF16)
-
         @pl.when(i == 0)
         def _():
             for k in (1, 2, 3):
                 wcopies[k].wait()
 
         acc[...] = xb[i].astype(F32) + bd[...] + bo[...]
-
-        def feed(j):
+        scores, probs, parts, hidden = {}, {}, {}, {}
+
+        def head_scores(h):
+            cols = pair_columns(h)
+            scores[h] = dot_nt(pick(bv[6, i, :, cols], h % 2), bv[5, i, :, cols])
+
+        def head_softmax(h):
+            value = scores.pop(h) + bias_v[...]
+            expo = jnp.exp(value - jnp.max(value, axis=0, keepdims=True))
+            probs[h] = (expo * (1.0 / jnp.sum(expo, axis=0, keepdims=True))).astype(BF16)
+            pb[i, h] = probs[h]
+
+        def head_context(h):
+            cols = pair_columns(h)
+            parts[h] = dot_tn(probs.pop(h), pick(bv[7, i, :, cols], h % 2))
+            if h % 2 == 1:
+                av[6, i, :, cols] = (parts.pop(h - 1) + parts.pop(h)).astype(BF16)
+
+        def feed_in(j):
             cols = slice(j * d, (j + 1) * d)
-            hidden = dot_nn(av[0, i], wi_v[:, cols]) + bi[:, cols]
-            gate = 0.5 * (1.0 + lax.erf(hidden * INV_ROOT_TWO))
-            act = (hidden * gate).astype(BF16)
-            av[1 + j, i] = act
-            bv[j, i] = (gate + hidden * jnp.exp(-0.5 * hidden * hidden) * INV_ROOT_TWO_PI).astype(BF16)
-            acc[...] += dot_nn(act, wo_v[j * d : (j + 1) * d, :])
-
-        both_parts(attend, feed)
+            hidden[j] = dot_nn(av[0, i], wi_v[:, cols]) + bi[:, cols]
+
+        def feed_gate(j):
+            value = hidden.pop(j)
+            gate = 0.5 * (1.0 + lax.erf(value * INV_ROOT_TWO))
+            av[1 + j, i] = (value * gate).astype(BF16)
+            bv[j, i] = (gate + value * jnp.exp(-0.5 * value * value) * INV_ROOT_TWO_PI).astype(BF16)
+
+        def feed_out(j):
+            acc[...] += dot_nn(av[1 + j, i], wo_v[j * d : (j + 1) * d, :])
+
+        pipelined(
+            ((0, head_scores), (2, head_softmax), (3, head_context)),
+            HEADS,
+            feed_slots(feed_in, feed_gate, feed_out),
+        )
         yb[i] = (acc[...] + dot_nn(av[6, i], wd_v[...])).astype(BF16)
 
         @pl.when(first)
@@ -252,39 +284,52 @@
         small[i, 7:8, :] = jnp.sum(gy.astype(F32), axis=0, keepdims=True)
         acc[...] = jnp.zeros_like(acc)
 
-        def feed(j):
-            cols = slice(j * d, (j + 1) * d)
-            dact = dot_nt(bv[4, i], wo_v[j * d : (j + 1) * d, :])
-            dh = (dact * bv[j, i].astype(F32)).astype(BF16)
+        dctx_v[...] = dot_nt(gy, wd_v[...]).astype(BF16)
+        dact, dprob, ds, dmix = {}, {}, {}, {}
+
+        def feed_in(j):
+            dact[j] = dot_nt(bv[4, i], wo_v[j * d : (j + 1) * d, :])
+
+        def feed_slope(j):
+            dh = (dact.pop(j) * bv[j, i].astype(F32)).astype(BF16)
             bv[j, i] = dh
             small[i, 8 + j : 9 + j, :] = jnp.sum(dh.astype(F32), axis=0, keepdims=True)
-            acc[...] += dot_nt(dh, wi_v[:, cols])
-
-        dctx_v[...] = dot_nt(gy, wd_v[...]).astype(BF16)
-
-        def attend(hp):
-            cols = slice(hp * 128, (hp + 1) * 128)
-            qp, kp, vp = bv[5, i, :, cols], bv[6, i, :, cols], bv[7, i, :, cols]
-            dop = dctx_v[:, cols]
-            dq = dk = dv = None
-            for a in range(2):
-                probs = pb[i, 2 * hp + a]
-                pf = probs.astype(F32)
-                dprob = dot_nt(pick(vp, a), dop)
-                prod = dprob * pf
-                ds = (prod - pf * jnp.sum(prod, axis=0, keepdims=True)).astype(BF16)
-                dv_a = dot_nn(probs, pick(dop, a))
-                dk_a = dot_nn(ds, pick(qp, a))
-                dq_a = dot_tn(ds, pick(kp, a))
-                dv = dv_a if dv is None else dv + dv_a
-                dk = dk_a if dk is None else dk + dk_a
-                dq = dq_a if dq is None else dq + dq_a
+
+        def feed_out(j):
+            acc[...] += dot_nt(bv[j, i], wi_v[:, j * d : (j + 1) * d])
+
+        def head_dprob(h):
+            cols = pair_columns(h)
+            dprob[h] = dot_nt(pick(bv[7, i, :, cols], h % 2), dctx_v[:, cols])
+
+        def head_dscores(h):
+            pf = pb[i, h].astype(F32)
+            prod = dprob.pop(h) * pf
+            ds[h] = (prod - pf * jnp.sum(prod, axis=0, keepdims=True)).astype(BF16)
+
+        def head_products(h):
+            cols = pair_columns(h)
+            value = ds.pop(h)
+            dv = dot_nn(pb[i, h], pick(dctx_v[:, cols], h % 2))
+            dk = dot_nn(value, pick(bv[5, i, :, cols], h % 2))
+            dq = dot_tn(value, pick(bv[6, i, :, cols], h % 2))
+            dmix[h] = (dq, dk, dv)
+
+        def pair_settle(h):
+            if h % 2 == 0:
+                return
+            cols = pair_columns(h)
+            dq, dk, dv = [p + q for p, q in zip(dmix.pop(h - 1), dmix.pop(h))]
             for t, w in ((0, rotate(dq * HEAD ** (-0.5), -1.0)), (1, rotate(dk, -1.0)), (2, dv)):
                 w = w.astype(BF16)
                 bv[5 + t, i, :, cols] = w
                 small[i, 4 + t : 5 + t, cols] = jnp.sum(w.astype(F32), axis=0, keepdims=True)
 
-        both_parts(attend, feed)
+        pipelined(
+            ((0, head_dprob), (2, head_dscores), (3, head_products), (4, pair_settle)),
+            HEADS,
+            feed_slots(feed_in, feed_slope, feed_out),
+        )
         da1 = dot_nt(bv[5, i], wqkv_v[:, 0:d])
         da1 = da1 + dot_nt(bv[6, i], wqkv_v[:, d : 2 * d])
         da1 = da1 + dot_nt(bv[7, i], wqkv_v[:, 2 * d : 3 * d])
@@ -425,10 +470,7 @@
     a_hbm,
     b_hbm,
     small,
-    out_in,
-    out_out,
-    out_qkv,
-    out_dense,
+    out_all,
     out_vec,
     out_nrm,
     abuf,
@@ -436,7 +478,6 @@
     own,
     csend,
     crecv,
-    fin,
     yred,
     leafy,
     leafz,
@@ -448,7 +489,6 @@
     nrm,
     nrecv,
     absem,
-    outsem,
     s_core,
     r_core,
     s_yred,
@@ -526,7 +566,7 @@
         return remote(own.at[b, z_mine], yz.at[b], s_yz.at[b], r_yz.at[b], y_peer)
 
     def piece(b, k):
-        return fin.at[b, half + k]
+        return out_all.at[b, half + k]
 
     def c_toty(b):
         return remote(piece(b, y_mine), piece(b, y_mine), s_toty.at[b], r_toty.at[b], near)
@@ -543,6 +583,9 @@
 
     def c_ag(b, k):
         return remote(piece(b, k), piece(b, k), s_ag.at[k, b], r_ag.at[k, b], core_peer)
+
+    def finish(b, k):
+        c_ag(b, k).start()
 
     vec_to = (core_peer, y_peer, near, across, near)
 
@@ -673,67 +716,40 @@
         @pl.when(mid)
         def _():
             c_yz(b).wait_recv()
-            fin[b, half + z_mine] = add(own[b, z_mine], yz[b]).astype(BF16)
+            out_all[b, half + z_mine] = add(own[b, z_mine], yz[b]).astype(BF16)
             c_totz(b).start()
             c_lz(b, 0).start()
-            c_ag(b, z_mine).start()
+            finish(b, z_mine)
             c_midy(b).wait_recv()
-            fin[b, half + y_mine] = add(own[b, y_mine], midy[b]).astype(BF16)
+            out_all[b, half + y_mine] = add(own[b, y_mine], midy[b]).astype(BF16)
             c_toty(b).start()
             c_boty(b).start()
-            c_ag(b, y_mine).start()
+            finish(b, y_mine)
 
     def lag5(b):
         @pl.when(mid)
         def _():
             c_totz(b).wait_recv()
             c_lz(b, 1).start()
-            c_ag(b, z_other).start()
+            finish(b, z_other)
             c_boty(b).wait_recv()
-            c_ag(b, y_other).start()
+            finish(b, y_other)
 
         @pl.when(leaf)
         def _():
             c_toty(b).wait_recv()
             c_boty(b).start()
-            c_ag(b, y_mine).start()
+            finish(b, y_mine)
             c_lz(b, 0).wait_recv()
-            c_ag(b, z_mine).start()
+            finish(b, z_mine)
 
     def lag6(b):
         @pl.when(leaf)
         def _():
             c_boty(b).wait_recv()
-            c_ag(b, y_other).start()
+            finish(b, y_other)
             c_lz(b, 1).wait_recv()
-            c_ag(b, z_other).start()
-
-    def out_copies(b, act):
-        w = b // SPLITS
-        rows = pl.ds((b % SPLITS) * 2 * PIECES, 2 * PIECES)
-
-        @pl.when(w // 4 == 0)
-        def _():
-            cols = pl.ds(pl.multiple_of(w * d, 128), d)
-            act(pltpu.make_async_copy(fin.at[b], out_in.at[rows, :, cols], outsem.at[b]))
-
-        @pl.when(w // 4 == 1)
-        def _():
-            act(pltpu.make_async_copy(fin.at[b], out_out.at[w - 4, rows], outsem.at[b]))
-
-        @pl.when((w // 4 == 2) & (w < 11))
-        def _():
-            cols = pl.ds(pl.multiple_of((w - 8) * d, 128), d)
-            act(pltpu.make_async_copy(fin.at[b], out_qkv.at[rows, :, cols], outsem.at[b]))
-
-        @pl.when(w == 11)
-        def _():
-            act(pltpu.make_async_copy(fin.at[b], out_dense.at[rows], outsem.at[b]))
-
-    def lag7(b):
-        for k in range(PIECES):
-            c_ag(b, k).wait_recv()
-        out_copies(b, lambda c: c.start())
+            finish(b, z_other)
 
     def vector_steps(t):
         @pl.when(t == 1)
@@ -773,7 +789,7 @@
         def _():
             c_nrm().start()
 
-    stages = (weight_block, lag1, lag2, lag3, lag4, lag5, lag6, lag7)
+    stages = (weight_block, lag1, lag2, lag3, lag4, lag5, lag6)
 
     def step(t, carry):
         for lag, stage in enumerate(stages):
@@ -808,7 +824,7 @@
         c_yred(b).wait_send()
         c_boty(b).wait_send()
         for k in range(PIECES):
-            c_ag(b, k).wait_send()
+            c_ag(b, k).wait()
 
         @pl.when(leaf)
         def _():
@@ -825,46 +841,38 @@
             c_lz(b, 0).wait_send()
             c_lz(b, 1).wait_send()
 
-        out_copies(b, lambda c: c.wait())
         return carry
 
     lax.fori_loop(0, nb, drain, 0)
 
 
-def gradient_call(a, b, small):
+def gradient_call(a, b, small, stay):
     n_mb, seq, d = a.shape[1:]
     nb = 12 * SPLITS
-    lead = 2 * PIECES * SPLITS
-    rows = d // lead
+    rows = d // (2 * PIECES * SPLITS)
+    summed = (nb, 2 * PIECES, rows, d)
     vmem = pl.BlockSpec(memory_space=pltpu.VMEM)
     hbm = pl.BlockSpec(memory_space=pl.ANY)
     dma = pltpu.SemaphoreType.DMA
 
-    def wide(columns):
-        return jax.ShapeDtypeStruct((lead, rows, columns), BF16)
-
     def slots(*lead):
         return pltpu.VMEM(lead + (rows, d), BF16)
 
     return pl.pallas_call(
         functools.partial(gradient_kernel, nb),
         out_shape=(
-            wide(4 * d),
-            jax.ShapeDtypeStruct((4, lead, rows, d), BF16),
-            wide(3 * d),
-            wide(d),
+            pltpu.VMEM(summed, BF16) if stay else jax.ShapeDtypeStruct(summed, BF16),
             jax.ShapeDtypeStruct((16, d), F32),
             jax.ShapeDtypeStruct((n_mb, 8, 128), F32),
         ),
         in_specs=[hbm, hbm, vmem],
-        out_specs=(hbm, hbm, hbm, hbm, vmem, vmem),
+        out_specs=(vmem, vmem, vmem),
         scratch_shapes=[
             pltpu.VMEM((2, n_mb, seq, d), BF16),
             pltpu.VMEM((2, n_mb, seq, d), BF16),
             slots(nb, PIECES),
             slots(2, PIECES),
             slots(nb, PIECES),
-            slots(nb, 2 * PIECES),
             slots(nb),
             slots(nb),
             slots(nb, 2),
@@ -876,14 +884,13 @@
             pltpu.VMEM((n_mb, 8, 128), F32),
             pltpu.VMEM((n_mb, 8, 128), F32),
             dma((2, 2)),
-            dma((nb,)),
             dma((2,)),
             dma((nb,)),
         ]
         + [dma((nb,)) for _ in range(18)]
         + [dma((2, nb)), dma((2, nb)), dma((PIECES, nb)), dma((PIECES, nb)), dma((5,)), dma((5,)), dma, dma],
         compiler_params=pltpu.CompilerParams(
-            collective_id=1, has_side_effects=True, vmem_limit_bytes=62 * 2**20
+            collective_id=1, has_side_effects=True, vmem_limit_bytes=(44 if stay else 60) * 2**20
         ),
         cost_estimate=pl.CostEstimate(
             flops=24 * n_mb * seq * d * d, bytes_accessed=64 * 2**20, transcendentals=0
@@ -891,35 +898,122 @@
     )(a, b, small)
 
 
+def widen_kernel(
+    blocks,
+    y_in,
+    dx_in,
+    vec,
+    nrm,
+    out_y,
+    out_dx,
+    gain1,
+    bias1,
+    w_qkv,
+    b_qkv,
+    w_dense,
+    b_dense,
+    gain2,
+    bias2,
+    w_in,
+    b_in,
+    w_out,
+    b_out,
+    norms,
+    narrow,
+    wide,
+    held,
+    isem,
+    osem,
+    csem,
+):
+    d = wide.shape[2]
+    reads = [
+        pltpu.make_async_copy(blocks.at[pl.ds(w * SPLITS, SPLITS)], narrow.at[w % 4], isem.at[w % 4])
+        for w in range(12)
+    ]
+    targets = [w_in.at[0, :, pl.ds(k * d, d)] for k in range(4)]
+    targets += [w_out.at[0, pl.ds(k * d, d)] for k in range(4)]
+    targets += [w_qkv.at[0, :, pl.ds(k * d, d)] for k in range(3)]
+    targets += [w_dense.at[0]]
+    writes = [pltpu.make_async_copy(wide.at[w], targets[w], osem.at[w]) for w in range(12)]
+    copies = [
+        pltpu.make_async_copy(held.at[0], out_y, csem.at[2]),
+        pltpu.make_async_copy(held.at[1], out_dx, csem.at[3]),
+    ]
+    fetch = [
+        pltpu.make_async_copy(y_in, held.at[0], csem.at[0]),
+        pltpu.make_async_copy(dx_in, held.at[1], csem.at[1]),
+    ]
+    for c in fetch + reads[:3]:
+        c.start()
+    for row, refs in ((0, (gain1,)), (1, (bias1,)), (2, (gain2,)), (3, (bias2,)), (7, (b_dense, b_out))):
+        for ref in refs:
+            ref[...] = vec[row : row + 1, :]
+    for k in range(3):
+        b_qkv[:, k * d : (k + 1) * d] = vec[4 + k : 5 + k, :]
+    for k in range(4):
+        b_in[:, k * d : (k + 1) * d] = vec[8 + k : 9 + k, :]
+    for m in range(nrm.shape[0]):
+        norms[m] = jnp.sum(nrm[m])
+    for w in range(12):
+        if w + 3 < 12:
+            reads[w + 3].start()
+        reads[w].wait()
+        wide[w] = narrow[w % 4].astype(F32).reshape(d, d)
+        writes[w].start()
+    for c in fetch:
+        c.wait()
+    for c in copies:
+        c.start()
+    for c in writes + copies:
+        c.wait()
+
+
+def widen_call(blocks, y, dx, vec, nrm):
+    d = y.shape[3]
+    vmem = pl.BlockSpec(memory_space=pltpu.VMEM)
+    hbm = pl.BlockSpec(memory_space=pl.ANY)
+    dma = pltpu.SemaphoreType.DMA
+
+    def row(k):
+        return jax.ShapeDtypeStruct((1, k * d), F32)
+
+    def matrix(r, c):
+        return jax.ShapeDtypeStruct((1, r * d, c * d), F32)
+
+    same = jax.ShapeDtypeStruct(y.shape, BF16)
+    return pl.pallas_call(
+        widen_kernel,
+        out_shape=(same, same, row(1), row(1), matrix(1, 3), row(3), matrix(1, 1), row(1))
+        + (row(1), row(1), matrix(1, 4), row(4), matrix(4, 1), row(1))
+        + (jax.ShapeDtypeStruct(nrm.shape[:1], F32),),
+        in_specs=[hbm, hbm, hbm, vmem, vmem],
+        out_specs=(hbm, hbm) + (vmem, vmem, hbm, vmem, hbm, vmem) * 2 + (pl.BlockSpec(memory_space=pltpu.SMEM),),
+        scratch_shapes=[
+            pltpu.VMEM((4, SPLITS) + blocks.shape[1:], BF16),
+            pltpu.VMEM((12, d, d), F32),
+            pltpu.VMEM((2,) + y.shape, BF16),
+            dma((4,)),
+            dma((12,)),
+            dma((4,)),
+        ],
+        compiler_params=pltpu.CompilerParams(vmem_limit_bytes=42 * 2**20),
+        cost_estimate=pl.CostEstimate(flops=12 * d * d, bytes_accessed=72 * d * d, transcendentals=0),
+    )(blocks, y, dx, vec, nrm)
+
+
 def on_device(size, inputs, cotangent, lengths, *params):
     n_mb, seq, d = inputs.shape
     tables = jnp.asarray(rotary_tables(seq))
     out_y, out_dx, a, b, small = section_call(lengths, inputs, cotangent, params, tables)
-    w_in, w_out, w_qkv, w_dense, vectors, nrm = gradient_call(a, b, small)
-    sums = [w_in, w_out, w_qkv, w_dense, vectors]
-    if size > 16:
+    stay = size == 16
+    blocks, vectors, nrm = gradient_call(a, b, small, stay)
+    if stay:
+        blocks = pltpu.with_memory_space_constraint(blocks, pltpu.VMEM)
+    else:
         groups = [[g * 16 + r for g in range(size // 16)] for r in range(16)]
-        sums = [lax.psum(v, "dp", axis_index_groups=groups) for v in sums]
-    w_in, w_out, w_qkv, w_dense, vectors = [v.astype(F32) for v in sums]
-    norms = jnp.sum(nrm, axis=(1, 2))
-    rows = [vectors[k : k + 1] for k in range(12)]
-    return (
-        out_y,
-        out_dx,
-        rows[0],
-        rows[1],
-        w_qkv.reshape(1, d, 3 * d),
-        vectors[4:7].reshape(1, 3 * d),
-        w_dense.reshape(1, d, d),
-        rows[7],
-        rows[2],
-        rows[3],
-        w_in.reshape(1, d, 4 * d),
-        vectors[8:12].reshape(1, 4 * d),
-        w_out.reshape(1, 4 * d, d),
-        rows[7],
-        norms,
-    )
+        blocks, vectors = [lax.psum(v, "dp", axis_index_groups=groups) for v in (blocks, vectors)]
+    return widen_call(blocks, out_y, out_dx, vectors, nrm)
 
 
 def solution(mesh):

time: 286 us -> 267 us (0.934)
  other arithmetic: 18 us -> 0 us
  local copies, waits for them, and re-layouts: 7.53 us -> 0 us
  Pallas kernels: 259 us -> 266 us
    reshape x4 -> x0, other arithmetic: 16.5 us -> none  [the longest x1 5.05 us: on_device(): w_in.reshape(1, d, 4 * d)]
    pallas_call x1 -> x2, Pallas kernels: 152 us -> 165 us  [the longest x1 152 us: gradient_call(): pl.pallas_call(functools.partial(gradient_kernel, nb), out_shape=(pltpu.V...]
    unnamed x21 -> x0, local copies, waits for them, and re-layouts: 6.02 us -> none
    pallas_call x1, Pallas kernels: 106 us -> 101 us  [section_call(): pl.pallas_call(functools.partial(section_kernel, n_mb), out_shape=(jax.Sh...]
where the time goes in v4:
time: 267 us
  Pallas kernels  266 us (100%)
    pallas_call x1, Pallas kernels, gradient_call(): pl.pallas_call(functools.partial(gradient_kernel, nb), out_shape=(pltpu.V...  152 us
    pallas_call x1, Pallas kernels, section_call(): pl.pallas_call(functools.partial(section_kernel, n_mb), out_shape=(jax.Sh...  101 us
    pallas_call x1, Pallas kernels, widen_call(): pl.pallas_call(widen_kernel, out_shape=(same, same, row(1), row(1), matri...  13.3 us

profile of v4, /device:TPU:0, one launch (start us, length us, event | category | flops | bytes accessed | tf_op | source)
XLA Modules:
  0.0 266.8 jit_solution(10045001621850460086)
XLA Ops:
  0.7 100.8 %shard_map.271 = (bf16[1,4,256,768]{3,2,1,0:T(8,128)(2,1)}, bf16[1,4,256,768]{3,2,1,0:T(8,128)(2,1)}, bf16[7,4,256,768]{3,2,1,0:T(8,128)(2,1)}, bf16[8,4,256,768]{3,2,1,0:T(8,128)(2,1)}, f32[4,16,768]{2,1,0:T(8,128)}) custom-call(s32[4]{0:T(128)} %lens.1, bf16[4,256,768]{2,1,0:T(8,128)(2,1)} %inputs.1, bf16[4,256,768]{2,1,0:T(8,128)(2,1)} %cot.1, ...), custom_call_target="tpu_custom_call" | custom-call | flops 28991029248 | bytes 41943040 | tf_op jit(solution)/shard_map/pallas_call | solution.py:409
  101.4 151.9 %shard_map.272 = (bf16[24,8,48,768]{3,2,1,0:T(8,128)(2,1)S(1)}, f32[16,768]{1,0:T(8,128)}, f32[4,8,128]{2,1,0:T(8,128)}) custom-call(bf16[7,4,256,768]{3,2,1,0:T(8,128)(2,1)} %get-tuple-element.23.a_hbm, bf16[8,4,256,768]{3,2,1,0:T(8,128)(2,1)} %get-tuple-element.24.b_hbm, f32[4,16,768]{2,1,0:T(8,128)} %get-tuple-element.25.small), custom_call_target="tpu_custom_call" | custom-call | flops 14495514624 | bytes 67108864 | tf_op jit(solution)/shard_map/pallas_call | solution.py:861
  253.4 13.3 %shard_map.273 = (bf16[1,4,256,768]{3,2,1,0:T(8,128)(2,1)}, bf16[1,4,256,768]{3,2,1,0:T(8,128)(2,1)}, f32[1,768]{1,0:T(1,128)}, f32[1,768]{1,0:T(1,128)}, f32[1,...) custom-call(bf16[24,8,48,768]{3,2,1,0:T(8,128)(2,1)S(1)} %get-tuple-, ...), custom_call_target="tpu_custom_call" | custom-call | flops 7077888 | bytes 42467328 | tf_op jit(solution)/shard_map/pallas_call | solution.py:985

commit v5 on v4

--- a/solution.py
+++ b/solution.py
@@ -110,10 +110,15 @@
 
     @pl.when(first)
     def _():
-        pltpu.make_async_copy(inputs, xb, insem).start()
+        pltpu.make_async_copy(inputs.at[0], xb.at[0], insem.at[0]).start()
 
     for c in wcopies:
         c.start()
+
+    @pl.when(first)
+    def _():
+        rest = pl.ds(1, n_mb - 1)
+        pltpu.make_async_copy(inputs.at[rest], xb.at[rest], insem.at[1]).start()
 
     @pl.when(last)
     def _():
@@ -122,6 +127,17 @@
     barrier = pltpu.get_barrier_semaphore()
     pl.semaphore_signal(barrier, inc=1, device_id={"pipe": peer}, device_id_type=MESH)
     pl.semaphore_wait(barrier, 1)
+
+    def half_copy(k):
+        rows = pl.ds(k * (seq // 2), seq // 2)
+        return pltpu.make_async_remote_copy(
+            src_ref=yb.at[0, rows],
+            dst_ref=xb.at[0, rows],
+            send_sem=fsend.at[k * n_mb],
+            recv_sem=frecv.at[k * n_mb],
+            device_id={"pipe": peer},
+            device_id_type=MESH,
+        )
 
     def fcopy(i):
         return pltpu.make_async_remote_copy(
@@ -143,20 +159,17 @@
             device_id_type=MESH,
         )
 
-    lane = lax.broadcasted_iota(jnp.int32, (seq, 128), 1)
-    lower = lane < HEAD
-
     def pick(value, a):
+        lower = lax.broadcasted_iota(jnp.int32, value.shape, 1) < HEAD
         return jnp.where(lower if a == 0 else jnp.logical_not(lower), value, jnp.zeros_like(value))
 
-    def rotate(w, sign):
-        return (
-            w * tables[0]
-            + sign * (pltpu.roll(w, ROT // 2, 1) * tables[1] + pltpu.roll(w, 128 - ROT // 2, 1) * tables[2])
-        )
-
-    def unit_of(i):
-        x = xb[i].astype(F32)
+    def rotate(w, sign, rows=slice(None)):
+        up = pltpu.roll(w, ROT // 2, 1) * tables[1, rows]
+        down = pltpu.roll(w, 128 - ROT // 2, 1) * tables[2, rows]
+        return w * tables[0, rows] + sign * (up + down)
+
+    def unit_of(i, rows=slice(None)):
+        x = xb[i, rows].astype(F32)
         center = x - jnp.mean(x, axis=-1, keepdims=True)
         inverse = lax.rsqrt(jnp.mean(center * center, axis=-1, keepdims=True) + EPSILON)
         return x, center * inverse, inverse
@@ -182,92 +195,105 @@
             slots[(5 * k) // 2] = runs
         return slots
 
-    def forward(i):
-        @pl.when(last)
-        def _():
-            fcopy(i).wait_recv()
-
-        x, unit, inverse = unit_of(i)
+    def forward(i, start, count, ready):
+        rows, keys = slice(start, start + count), slice(0, start + count)
+        x, unit, inverse = unit_of(i, rows)
         a1 = (unit * g1[...] + b1[...]).astype(BF16)
-        a2 = (unit * g2[...] + b2[...]).astype(BF16)
-        av[5, i] = a1
-        av[0, i] = a2
-
-        @pl.when(i == 0)
-        def _():
-            wcopies[0].wait()
-
-        mixed = {}
+        av[5, i, rows] = a1
+        av[0, i, rows] = (unit * g2[...] + b2[...]).astype(BF16)
+        acc[rows] = x + bd[...] + bo[...]
+        if start == 0:
+            key = lax.broadcasted_iota(jnp.int32, (seq, seq), 0)
+            query = lax.broadcasted_iota(jnp.int32, (seq, seq), 1)
+            bias_v[...] = jnp.where((key <= query) & (key < lens[i]), 0.0, NEG_FILL)
+        mixed, scores, probs, parts, hidden = {}, {}, {}, {}, {}
 
         def project(t):
             mixed[t] = dot_nn(a1, wqkv_v[:, t * d : (t + 1) * d]) + bqkv[:, t * d : (t + 1) * d]
 
         def settle(t):
             if t == 2:
-                bv[7, i] = mixed[2].astype(BF16)
+                bv[7, i, rows] = mixed[2].astype(BF16)
                 return
             for hp in range(pairs):
-                w = rotate(mixed[t][:, hp * 128 : (hp + 1) * 128], 1.0)
+                w = rotate(mixed[t][:, hp * 128 : (hp + 1) * 128], 1.0, rows)
                 if t == 0:
                     w = w * HEAD ** (-0.5)
-                bv[5 + t, i, :, hp * 128 : (hp + 1) * 128] = w.astype(BF16)
-
-        pipelined(((0, project), (1, settle)), 3, {})
-        key = lax.broadcasted_iota(jnp.int32, (seq, seq), 0)
-        query = lax.broadcasted_iota(jnp.int32, (seq, seq), 1)
-        bias_v[...] = jnp.where((key <= query) & (key < lens[i]), 0.0, NEG_FILL)
-
-        @pl.when(i == 0)
-        def _():
-            for k in (1, 2, 3):
-                wcopies[k].wait()
-
-        acc[...] = xb[i].astype(F32) + bd[...] + bo[...]
-        scores, probs, parts, hidden = {}, {}, {}, {}
+                bv[5 + t, i, rows, hp * 128 : (hp + 1) * 128] = w.astype(BF16)
 
         def head_scores(h):
             cols = pair_columns(h)
-            scores[h] = dot_nt(pick(bv[6, i, :, cols], h % 2), bv[5, i, :, cols])
+            scores[h] = dot_nt(pick(bv[6, i, keys, cols], h % 2), bv[5, i, rows, cols])
 
         def head_softmax(h):
-            value = scores.pop(h) + bias_v[...]
+            value = scores.pop(h) + bias_v[keys, rows]
             expo = jnp.exp(value - jnp.max(value, axis=0, keepdims=True))
             probs[h] = (expo * (1.0 / jnp.sum(expo, axis=0, keepdims=True))).astype(BF16)
-            pb[i, h] = probs[h]
+            pb[i, h, keys, rows] = probs[h]
+            if start + count < seq:
+                pb[i, h, start + count :, rows] = jnp.zeros((seq - start - count, count), BF16)
 
         def head_context(h):
             cols = pair_columns(h)
-            parts[h] = dot_tn(probs.pop(h), pick(bv[7, i, :, cols], h % 2))
+            parts[h] = dot_tn(probs.pop(h), pick(bv[7, i, keys, cols], h % 2))
             if h % 2 == 1:
-                av[6, i, :, cols] = (parts.pop(h - 1) + parts.pop(h)).astype(BF16)
+                av[6, i, rows, cols] = (parts.pop(h - 1) + parts.pop(h)).astype(BF16)
 
         def feed_in(j):
             cols = slice(j * d, (j + 1) * d)
-            hidden[j] = dot_nn(av[0, i], wi_v[:, cols]) + bi[:, cols]
+            hidden[j] = dot_nn(av[0, i, rows], wi_v[:, cols]) + bi[:, cols]
 
         def feed_gate(j):
             value = hidden.pop(j)
             gate = 0.5 * (1.0 + lax.erf(value * INV_ROOT_TWO))
-            av[1 + j, i] = (value * gate).astype(BF16)
-            bv[j, i] = (gate + value * jnp.exp(-0.5 * value * value) * INV_ROOT_TWO_PI).astype(BF16)
+            av[1 + j, i, rows] = (value * gate).astype(BF16)
+            bv[j, i, rows] = (gate + value * jnp.exp(-0.5 * value * value) * INV_ROOT_TWO_PI).astype(BF16)
 
         def feed_out(j):
-            acc[...] += dot_nn(av[1 + j, i], wo_v[j * d : (j + 1) * d, :])
-
-        pipelined(
-            ((0, head_scores), (2, head_softmax), (3, head_context)),
-            HEADS,
-            feed_slots(feed_in, feed_gate, feed_out),
-        )
-        yb[i] = (acc[...] + dot_nn(av[6, i], wd_v[...])).astype(BF16)
-
-        @pl.when(first)
-        def _():
-            fcopy(i).start()
-
+            acc[rows] += dot_nn(av[1 + j, i, rows], wo_v[j * d : (j + 1) * d, :])
+
+        ready(0)
+        pipelined(((0, project), (1, settle)), 3, {})
+        heads = ((0, head_scores), (4, head_softmax), (6, head_context))
+        ready(1)
+        pipelined(heads, HEADS, feed_slots(feed_in, feed_gate, feed_out))
+        yb[i, rows] = (acc[rows] + dot_nn(av[6, i, rows], wd_v[...])).astype(BF16)
+
+    def forward_done(i):
         pltpu.make_async_copy(yb.at[i], out_y.at[0, i], ysem.at[i]).start()
         for k in range(7):
             pltpu.make_async_copy(av.at[k, i], a_hbm.at[k, i], asem.at[k, i]).start()
+
+    def forward_whole(i):
+        @pl.when(last)
+        def _():
+            fcopy(i).wait_recv()
+
+        forward(i, 0, seq, lambda k: None)
+
+        @pl.when(first)
+        def _():
+            fcopy(i).start()
+
+        forward_done(i)
+
+    def forward_halves():
+        def ready(k):
+            for c in wcopies[:1] if k == 0 else wcopies[1:]:
+                c.wait()
+
+        for k in range(2):
+            @pl.when(last)
+            def _(k=k):
+                half_copy(k).wait_recv()
+
+            forward(0, k * (seq // 2), seq // 2, ready if k == 0 else lambda k: None)
+
+            @pl.when(first)
+            def _(k=k):
+                half_copy(k).start()
+
+        forward_done(0)
 
     def backward(i):
         @pl.when(first)
@@ -330,9 +356,8 @@
             HEADS,
             feed_slots(feed_in, feed_slope, feed_out),
         )
-        da1 = dot_nt(bv[5, i], wqkv_v[:, 0:d])
-        da1 = da1 + dot_nt(bv[6, i], wqkv_v[:, d : 2 * d])
-        da1 = da1 + dot_nt(bv[7, i], wqkv_v[:, 2 * d : 3 * d])
+        dmixed = jnp.concatenate([bv[5, i], bv[6, i], bv[7, i]], axis=1)
+        da1 = dot_nt(dmixed, wqkv_v[...])
         da2 = acc[...]
         x, unit, inverse = unit_of(i)
         small[i, 0:1, :] = jnp.sum(da1 * unit, axis=0, keepdims=True)
@@ -355,19 +380,27 @@
 
     @pl.when(first)
     def _():
-        pltpu.make_async_copy(inputs, xb, insem).wait()
+        pltpu.make_async_copy(inputs.at[0], xb.at[0], insem.at[0]).wait()
+
+    forward_halves()
+
+    @pl.when(first)
+    def _():
+        rest = pl.ds(1, n_mb - 1)
+        pltpu.make_async_copy(inputs.at[rest], xb.at[rest], insem.at[1]).wait()
 
     @pl.when(last)
     def _():
         pltpu.make_async_copy(cot, bv.at[4], cotsem).wait()
 
     def tick(step, carry):
-        phase = section * (step % 2) + (1 - section) * (step // n_mb)
-        mb = section * (step // 2) + (1 - section) * (step % n_mb)
+        after = step + 1
+        phase = section * (after % 2) + (1 - section) * (after // n_mb)
+        mb = section * (after // 2) + (1 - section) * (after % n_mb)
 
         @pl.when(phase == 0)
         def _():
-            forward(mb)
+            forward_whole(mb)
 
         @pl.when(phase == 1)
         def _():
@@ -375,10 +408,10 @@
 
         return carry
 
-    lax.fori_loop(0, 2 * n_mb, tick, 0)
+    lax.fori_loop(0, 2 * n_mb - 1, tick, 0)
 
     def drain(i, carry):
-        @pl.when(first)
+        @pl.when(first & (i > 0))
         def _():
             fcopy(i).wait_send()
 
@@ -395,6 +428,11 @@
         return carry
 
     lax.fori_loop(0, n_mb, drain, 0)
+
+    @pl.when(first)
+    def _():
+        half_copy(0).wait_send()
+        half_copy(1).wait_send()
 
 
 def section_call(lens, inputs, cot, params, tables):
@@ -432,14 +470,14 @@
             pltpu.VMEM((seq, d), BF16),
             pltpu.VMEM((seq, seq), F32),
             dma((4,)),
-            dma,
+            dma((2,)),
             dma,
             dma((n_mb,)),
             dma((n_mb,)),
             dma((7, n_mb)),
             dma((8, n_mb)),
-            dma((n_mb,)),
-            dma((n_mb,)),
+            dma((n_mb + 1,)),
+            dma((n_mb + 1,)),
             dma((n_mb,)),
             dma((n_mb,)),
         ],
@@ -792,7 +830,8 @@
     stages = (weight_block, lag1, lag2, lag3, lag4, lag5, lag6)
 
     def step(t, carry):
-        for lag, stage in enumerate(stages):
+        for lag in (1, 0, 2, 3, 4, 5, 6):
+            stage = stages[lag]
 
             @pl.when((t >= lag) & (t - lag < nb))
             def _(lag=lag, stage=stage):
@@ -899,6 +938,7 @@
 
 
 def widen_kernel(
+    stay,
     blocks,
     y_in,
     dx_in,
@@ -936,15 +976,22 @@
     targets += [w_qkv.at[0, :, pl.ds(k * d, d)] for k in range(3)]
     targets += [w_dense.at[0]]
     writes = [pltpu.make_async_copy(wide.at[w], targets[w], osem.at[w]) for w in range(12)]
-    copies = [
-        pltpu.make_async_copy(held.at[0], out_y, csem.at[2]),
-        pltpu.make_async_copy(held.at[1], out_dx, csem.at[3]),
-    ]
-    fetch = [
-        pltpu.make_async_copy(y_in, held.at[0], csem.at[0]),
-        pltpu.make_async_copy(dx_in, held.at[1], csem.at[1]),
-    ]
-    for c in fetch + reads[:3]:
+    if stay:
+        copies = [
+            pltpu.make_async_copy(y_in, out_y, csem.at[2]),
+            pltpu.make_async_copy(dx_in, out_dx, csem.at[3]),
+        ]
+        fetch = []
+    else:
+        copies = [
+            pltpu.make_async_copy(held.at[0], out_y, csem.at[2]),
+            pltpu.make_async_copy(held.at[1], out_dx, csem.at[3]),
+        ]
+        fetch = [
+            pltpu.make_async_copy(y_in, held.at[0], csem.at[0]),
+            pltpu.make_async_copy(dx_in, held.at[1], csem.at[1]),
+        ]
+    for c in (copies if stay else fetch) + reads[:3]:
         c.start()
     for row, refs in ((0, (gain1,)), (1, (bias1,)), (2, (gain2,)), (3, (bias2,)), (7, (b_dense, b_out))):
         for ref in refs:
@@ -963,13 +1010,13 @@
         writes[w].start()
     for c in fetch:
         c.wait()
-    for c in copies:
+    for c in [] if stay else copies:
         c.start()
     for c in writes + copies:
         c.wait()
 
 
-def widen_call(blocks, y, dx, vec, nrm):
+def widen_call(blocks, y, dx, vec, nrm, stay):
     d = y.shape[3]
     vmem = pl.BlockSpec(memory_space=pltpu.VMEM)
     hbm = pl.BlockSpec(memory_space=pl.ANY)
@@ -983,7 +1030,7 @@
 
     same = jax.ShapeDtypeStruct(y.shape, BF16)
     return pl.pallas_call(
-        widen_kernel,
+        functools.partial(widen_kernel, stay),
         out_shape=(same, same, row(1), row(1), matrix(1, 3), row(3), matrix(1, 1), row(1))
         + (row(1), row(1), matrix(1, 4), row(4), matrix(4, 1), row(1))
         + (jax.ShapeDtypeStruct(nrm.shape[:1], F32),),
@@ -992,7 +1039,7 @@
         scratch_shapes=[
             pltpu.VMEM((4, SPLITS) + blocks.shape[1:], BF16),
             pltpu.VMEM((12, d, d), F32),
-            pltpu.VMEM((2,) + y.shape, BF16),
+            pltpu.VMEM((1, 8, 128) if stay else (2,) + y.shape, BF16),
             dma((4,)),
             dma((12,)),
             dma((4,)),
@@ -1009,11 +1056,13 @@
     stay = size == 16
     blocks, vectors, nrm = gradient_call(a, b, small, stay)
     if stay:
-        blocks = pltpu.with_memory_space_constraint(blocks, pltpu.VMEM)
+        blocks, out_y, out_dx = [
+            pltpu.with_memory_space_constraint(v, pltpu.VMEM) for v in (blocks, out_y, out_dx)
+        ]
     else:
         groups = [[g * 16 + r for g in range(size // 16)] for r in range(16)]
         blocks, vectors = [lax.psum(v, "dp", axis_index_groups=groups) for v in (blocks, vectors)]
-    return widen_call(blocks, out_y, out_dx, vectors, nrm)
+    return widen_call(blocks, out_y, out_dx, vectors, nrm, stay)
 
 
 def solution(mesh):

time: 267 us -> 253 us (0.948)
  Pallas kernels: 266 us -> 252 us
    pallas_call x1, Pallas kernels: 101 us -> 90.6 us  [section_call(): pl.pallas_call(functools.partial(section_kernel, n_mb), out_shape=(jax.Sh...]
    pallas_call x1, Pallas kernels: 152 us -> 149 us  [gradient_call(): pl.pallas_call(functools.partial(gradient_kernel, nb), out_shape=(pltpu.V...]
where the time goes in v5:
time: 253 us; the launch traced here: 252 us
  Pallas kernels  252 us (100%)
    pallas_call x1, Pallas kernels, gradient_call(): pl.pallas_call(functools.partial(gradient_kernel, nb), out_shape=(pltpu.V...  149 us
    pallas_call x1, Pallas kernels, section_call(): pl.pallas_call(functools.partial(section_kernel, n_mb), out_shape=(jax.Sh...  90.6 us
    pallas_call x1, Pallas kernels, widen_call(): pl.pallas_call(functools.partial(widen_kernel, stay), out_shape=(same, sa...  12.3 us

profile of v5, /device:TPU:0, one launch (start us, length us, event | category | flops | bytes accessed | tf_op | source)
XLA Modules:
  0.0 252.5 jit_solution(14204414774666600738)
XLA Ops:
  0.7 90.6 %shard_map.271 = (bf16[1,4,256,768]{3,2,1,0:T(8,128)(2,1)}, bf16[1,4,256,768]{3,2,1,0:T(8,128)(2,1)}, bf16[7,4,256,768]{3,2,1,0:T(8,128)(2,1)}, bf16[8,4,256,768]{3,2,1,0:T(8,128)(2,1)}, f32[4,16,768]{2,1,0:T(8,128)}) custom-call(s32[4]{0:T(128)} %lens.1, bf16[4,256,768]{2,1,0:T(8,128)(2,1)} %inputs.1, bf16[4,256,768]{2,1,0:T(8,128)(2,1)} %cot.1, ...), custom_call_target="tpu_custom_call" | custom-call | flops 28991029248 | bytes 41943040 | tf_op jit(solution)/shard_map/pallas_call | solution.py:447
  91.2 0.0 copy-start
  91.2 0.0 copy-start.1
  91.2 148.7 %shard_map.272 = (bf16[24,8,48,768]{3,2,1,0:T(8,128)(2,1)S(1)}, f32[16,768]{1,0:T(8,128)}, f32[4,8,128]{2,1,0:T(8,128)}) custom-call(bf16[7,4,256,768]{3,2,1,0:T(8,128)(2,1)} %get-tuple-element.23.a_hbm, bf16[8,4,256,768]{3,2,1,0:T(8,128)(2,1)} %get-tuple-element.24.b_hbm, f32[4,16,768]{2,1,0:T(8,128)} %get-tuple-element.25.small), custom_call_target="tpu_custom_call" | custom-call | flops 14495514624 | bytes 67108864 | tf_op jit(solution)/shard_map/pallas_call | solution.py:900
  240.0 0.0 copy-done
  240.0 0.0 copy-done.1
  240.0 12.3 %shard_map.273 = (bf16[1,4,256,768]{3,2,1,0:T(8,128)(2,1)}, bf16[1,4,256,768]{3,2,1,0:T(8,128)(2,1)}, f32[1,768]{1,0:T(1,128)}, f32[1,768]{1,0:T(1,128)}, f32[1,...) custom-call(bf16[24,8,48,768]{3,2,1,0:T(8,128)(2,1)S(1)} %get-tuple-, ...), custom_call_target="tpu_custom_call" | custom-call | flops 7077888 | bytes 42467328 | tf_op jit(solution)/shard_map/pallas_call | solution.py:1032
Async XLA Ops:
  91.2 148.8 %copy-start = (bf16[1,4,256,768]{3,2,1,0:T(8,128)(2,1)S(1)}, bf16[1,4,256,768]{3,2,1,0:T(8,128)(2,1)}, u32[]{:S(2)}) copy-start(bf16[1,4,256,768]{3,2,1,0:T(8,128)(2,1)} %get-tuple-element.27.y_in) | copy-start | bytes 4718596
  91.2 148.8 %copy-start.1 = (bf16[1,4,256,768]{3,2,1,0:T(8,128)(2,1)S(1)}, bf16[1,4,256,768]{3,2,1,0:T(8,128)(2,1)}, u32[]{:S(2)}) copy-start(bf16[1,4,256,768]{3,2,1,0:T(8,128)(2,1)} %get-tuple-element.28.dx_in) | copy-start | bytes 4718596

commit v6 on v5

--- a/solution.py
+++ b/solution.py
@@ -105,8 +105,14 @@
 
     wcopies = [
         pltpu.make_async_copy(src.at[0], dst, wsem.at[k])
-        for k, (src, dst) in enumerate(((wqkv, wqkv_v), (wd, wd_v), (wi, wi_v), (wo, wo_v)))
+        for k, (src, dst) in enumerate(((wd, wd_v), (wi, wi_v), (wo, wo_v)))
     ]
+    wcopies = [
+        pltpu.make_async_copy(
+            wqkv.at[0, :, pl.ds(t * d, d)], wqkv_v.at[:, pl.ds(t * d, d)], wsem.at[3 + t]
+        )
+        for t in range(3)
+    ] + wcopies
 
     @pl.when(first)
     def _():
@@ -185,14 +191,14 @@
                 if 0 <= t - lag < count:
                     stage(t - lag)
 
-    def feed_slots(feed_in, feed_mid, feed_out):
+    def feed_slots(feed_in, feed_mid, feed_out, place):
         slots = {}
         for k in range(6):
             runs = []
             for lag, stage in ((2, feed_out), (1, feed_mid), (0, feed_in)):
                 if 0 <= k - lag < 4:
                     runs.append(functools.partial(stage, k - lag))
-            slots[(5 * k) // 2] = runs
+            slots.setdefault(place(k), []).extend(runs)
         return slots
 
     def forward(i, start, count, ready):
@@ -209,6 +215,7 @@
         mixed, scores, probs, parts, hidden = {}, {}, {}, {}, {}
 
         def project(t):
+            ready(t)
             mixed[t] = dot_nn(a1, wqkv_v[:, t * d : (t + 1) * d]) + bqkv[:, t * d : (t + 1) * d]
 
         def settle(t):
@@ -252,11 +259,10 @@
         def feed_out(j):
             acc[rows] += dot_nn(av[1 + j, i, rows], wo_v[j * d : (j + 1) * d, :])
 
-        ready(0)
         pipelined(((0, project), (1, settle)), 3, {})
         heads = ((0, head_scores), (4, head_softmax), (6, head_context))
-        ready(1)
-        pipelined(heads, HEADS, feed_slots(feed_in, feed_gate, feed_out))
+        ready(3)
+        pipelined(heads, HEADS, feed_slots(feed_in, feed_gate, feed_out, lambda k: 2 + 3 * k))
         yb[i, rows] = (acc[rows] + dot_nn(av[6, i, rows], wd_v[...])).astype(BF16)
 
     def forward_done(i):
@@ -279,7 +285,7 @@
 
     def forward_halves():
         def ready(k):
-            for c in wcopies[:1] if k == 0 else wcopies[1:]:
+            for c in wcopies[k : k + 1] if k < 3 else wcopies[3:]:
                 c.wait()
 
         for k in range(2):
@@ -308,8 +314,6 @@
 
         gy = bv[4, i]
         small[i, 7:8, :] = jnp.sum(gy.astype(F32), axis=0, keepdims=True)
-        acc[...] = jnp.zeros_like(acc)
-
         dctx_v[...] = dot_nt(gy, wd_v[...]).astype(BF16)
         dact, dprob, ds, dmix = {}, {}, {}, {}
 
@@ -322,7 +326,8 @@
             small[i, 8 + j : 9 + j, :] = jnp.sum(dh.astype(F32), axis=0, keepdims=True)
 
         def feed_out(j):
-            acc[...] += dot_nt(bv[j, i], wi_v[:, j * d : (j + 1) * d])
+            part = dot_nt(bv[j, i], wi_v[:, j * d : (j + 1) * d])
+            acc[...] = part if j == 0 else acc[...] + part
 
         def head_dprob(h):
             cols = pair_columns(h)
@@ -354,16 +359,18 @@
         pipelined(
             ((0, head_dprob), (2, head_dscores), (3, head_products), (4, pair_settle)),
             HEADS,
-            feed_slots(feed_in, feed_slope, feed_out),
+            feed_slots(feed_in, feed_slope, feed_out, lambda k: 2 + 2 * k),
         )
+        for k in range(8):
+            pltpu.make_async_copy(bv.at[k, i], b_hbm.at[k, i], bsem.at[k, i]).start()
+        x, unit, inverse = unit_of(i)
+        da2 = acc[...]
+        small[i, 2:3, :] = jnp.sum(da2 * unit, axis=0, keepdims=True)
+        small[i, 3:4, :] = jnp.sum(da2, axis=0, keepdims=True)
         dmixed = jnp.concatenate([bv[5, i], bv[6, i], bv[7, i]], axis=1)
         da1 = dot_nt(dmixed, wqkv_v[...])
-        da2 = acc[...]
-        x, unit, inverse = unit_of(i)
         small[i, 0:1, :] = jnp.sum(da1 * unit, axis=0, keepdims=True)
         small[i, 1:2, :] = jnp.sum(da1, axis=0, keepdims=True)
-        small[i, 2:3, :] = jnp.sum(da2 * unit, axis=0, keepdims=True)
-        small[i, 3:4, :] = jnp.sum(da2, axis=0, keepdims=True)
         scaled = da1 * g1[...] + da2 * g2[...]
         mean_g = jnp.mean(scaled, axis=-1, keepdims=True)
         mean_gn = jnp.mean(scaled * unit, axis=-1, keepdims=True)
@@ -375,8 +382,6 @@
             bcopy(i).start()
 
         pltpu.make_async_copy(dxb.at[i], out_dx.at[0, i], dxsem.at[i]).start()
-        for k in range(8):
-            pltpu.make_async_copy(bv.at[k, i], b_hbm.at[k, i], bsem.at[k, i]).start()
 
     @pl.when(first)
     def _():
@@ -469,7 +474,7 @@
             pltpu.VMEM((seq, d), F32),
             pltpu.VMEM((seq, d), BF16),
             pltpu.VMEM((seq, seq), F32),
-            dma((4,)),
+            dma((6,)),
             dma((2,)),
             dma,
             dma((n_mb,)),

time: 253 us -> 251 us (level)
  no operation moved by 1% of the time
where the time goes in v6:
time: 251 us
  Pallas kernels  250 us (100%)
    pallas_call x1, Pallas kernels, gradient_call(): pl.pallas_call(functools.partial(gradient_kernel, nb), out_shape=(pltpu.V...  149 us
    pallas_call x1, Pallas kernels, section_call(): pl.pallas_call(functools.partial(section_kernel, n_mb), out_shape=(jax.Sh...  88.9 us
    pallas_call x1, Pallas kernels, widen_call(): pl.pallas_call(functools.partial(widen_kernel, stay), out_shape=(same, sa...  12.3 us

profile of v6, /device:TPU:0, one launch (start us, length us, event | category | flops | bytes accessed | tf_op | source)
XLA Modules:
  0.0 250.7 jit_solution(7133138404326697351)
XLA Ops:
  0.7 88.9 %shard_map.271 = (bf16[1,4,256,768]{3,2,1,0:T(8,128)(2,1)}, bf16[1,4,256,768]{3,2,1,0:T(8,128)(2,1)}, bf16[7,4,256,768]{3,2,1,0:T(8,128)(2,1)}, bf16[8,4,256,768]{3,2,1,0:T(8,128)(2,1)}, f32[4,16,768]{2,1,0:T(8,128)}) custom-call(s32[4]{0:T(128)} %lens.1, bf16[4,256,768]{2,1,0:T(8,128)(2,1)} %inputs.1, bf16[4,256,768]{2,1,0:T(8,128)(2,1)} %cot.1, ...), custom_call_target="tpu_custom_call" | custom-call | flops 28991029248 | bytes 41943040 | tf_op jit(solution)/shard_map/pallas_call | solution.py:452
  89.6 0.0 copy-start
  89.6 0.0 copy-start.1
  89.6 148.6 %shard_map.272 = (bf16[24,8,48,768]{3,2,1,0:T(8,128)(2,1)S(1)}, f32[16,768]{1,0:T(8,128)}, f32[4,8,128]{2,1,0:T(8,128)}) custom-call(bf16[7,4,256,768]{3,2,1,0:T(8,128)(2,1)} %get-tuple-element.23.a_hbm, bf16[8,4,256,768]{3,2,1,0:T(8,128)(2,1)} %get-tuple-element.24.b_hbm, f32[4,16,768]{2,1,0:T(8,128)} %get-tuple-element.25.small), custom_call_target="tpu_custom_call" | custom-call | flops 14495514624 | bytes 67108864 | tf_op jit(solution)/shard_map/pallas_call | solution.py:905
  238.2 0.0 copy-done
  238.2 0.0 copy-done.1
  238.2 12.3 %shard_map.273 = (bf16[1,4,256,768]{3,2,1,0:T(8,128)(2,1)}, bf16[1,4,256,768]{3,2,1,0:T(8,128)(2,1)}, f32[1,768]{1,0:T(1,128)}, f32[1,768]{1,0:T(1,128)}, f32[1,...) custom-call(bf16[24,8,48,768]{3,2,1,0:T(8,128)(2,1)S(1)} %get-tuple-, ...), custom_call_target="tpu_custom_call" | custom-call | flops 7077888 | bytes 42467328 | tf_op jit(solution)/shard_map/pallas_call | solution.py:1037
Async XLA Ops:
  89.6 148.6 %copy-start = (bf16[1,4,256,768]{3,2,1,0:T(8,128)(2,1)S(1)}, bf16[1,4,256,768]{3,2,1,0:T(8,128)(2,1)}, u32[]{:S(2)}) copy-start(bf16[1,4,256,768]{3,2,1,0:T(8,128)(2,1)} %get-tuple-element.27.y_in) | copy-start | bytes 4718596
  89.6 148.6 %copy-start.1 = (bf16[1,4,256,768]{3,2,1,0:T(8,128)(2,1)S(1)}, bf16[1,4,256,768]{3,2,1,0:T(8,128)(2,1)}, u32[]{:S(2)}) copy-start(bf16[1,4,256,768]{3,2,1,0:T(8,128)(2,1)} %get-tuple-element.28.dx_in) | copy-start | bytes 4718596

commit v7 on v6

--- a/solution.py
+++ b/solution.py
@@ -359,7 +359,7 @@
         pipelined(
             ((0, head_dprob), (2, head_dscores), (3, head_products), (4, pair_settle)),
             HEADS,
-            feed_slots(feed_in, feed_slope, feed_out, lambda k: 2 + 2 * k),
+            feed_slots(feed_in, feed_slope, feed_out, lambda k: 4 + 2 * k),
         )
         for k in range(8):
             pltpu.make_async_copy(bv.at[k, i], b_hbm.at[k, i], bsem.at[k, i]).start()

time: 251 us -> 251 us (level)
  no operation moved by 1% of the time
where the time goes in v7:
time: 251 us; the launch traced here: 250 us
  Pallas kernels  250 us (100%)
    pallas_call x1, Pallas kernels, gradient_call(): pl.pallas_call(functools.partial(gradient_kernel, nb), out_shape=(pltpu.V...  149 us
    pallas_call x1, Pallas kernels, section_call(): pl.pallas_call(functools.partial(section_kernel, n_mb), out_shape=(jax.Sh...  88.7 us
    pallas_call x1, Pallas kernels, widen_call(): pl.pallas_call(functools.partial(widen_kernel, stay), out_shape=(same, sa...  12.3 us

profile of v7, /device:TPU:0, one launch (start us, length us, event | category | flops | bytes accessed | tf_op | source)
XLA Modules:
  0.0 250.5 jit_solution(11117848224615964007)
XLA Ops:
  0.7 88.7 %shard_map.271 = (bf16[1,4,256,768]{3,2,1,0:T(8,128)(2,1)}, bf16[1,4,256,768]{3,2,1,0:T(8,128)(2,1)}, bf16[7,4,256,768]{3,2,1,0:T(8,128)(2,1)}, bf16[8,4,256,768]{3,2,1,0:T(8,128)(2,1)}, f32[4,16,768]{2,1,0:T(8,128)}) custom-call(s32[4]{0:T(128)} %lens.1, bf16[4,256,768]{2,1,0:T(8,128)(2,1)} %inputs.1, bf16[4,256,768]{2,1,0:T(8,128)(2,1)} %cot.1, ...), custom_call_target="tpu_custom_call" | custom-call | flops 28991029248 | bytes 41943040 | tf_op jit(solution)/shard_map/pallas_call | solution.py:452
  89.4 0.0 copy-start
  89.4 0.0 copy-start.1
  89.4 148.6 %shard_map.272 = (bf16[24,8,48,768]{3,2,1,0:T(8,128)(2,1)S(1)}, f32[16,768]{1,0:T(8,128)}, f32[4,8,128]{2,1,0:T(8,128)}) custom-call(bf16[7,4,256,768]{3,2,1,0:T(8,128)(2,1)} %get-tuple-element.23.a_hbm, bf16[8,4,256,768]{3,2,1,0:T(8,128)(2,1)} %get-tuple-element.24.b_hbm, f32[4,16,768]{2,1,0:T(8,128)} %get-tuple-element.25.small), custom_call_target="tpu_custom_call" | custom-call | flops 14495514624 | bytes 67108864 | tf_op jit(solution)/shard_map/pallas_call | solution.py:905
  238.0 0.0 copy-done
  238.0 0.0 copy-done.1
  238.0 12.3 %shard_map.273 = (bf16[1,4,256,768]{3,2,1,0:T(8,128)(2,1)}, bf16[1,4,256,768]{3,2,1,0:T(8,128)(2,1)}, f32[1,768]{1,0:T(1,128)}, f32[1,768]{1,0:T(1,128)}, f32[1,...) custom-call(bf16[24,8,48,768]{3,2,1,0:T(8,128)(2,1)S(1)} %get-tuple-, ...), custom_call_target="tpu_custom_call" | custom-call | flops 7077888 | bytes 42467328 | tf_op jit(solution)/shard_map/pallas_call | solution.py:1037
Async XLA Ops:
  89.4 148.6 %copy-start = (bf16[1,4,256,768]{3,2,1,0:T(8,128)(2,1)S(1)}, bf16[1,4,256,768]{3,2,1,0:T(8,128)(2,1)}, u32[]{:S(2)}) copy-start(bf16[1,4,256,768]{3,2,1,0:T(8,128)(2,1)} %get-tuple-element.27.y_in) | copy-start | bytes 4718596
  89.4 148.6 %copy-start.1 = (bf16[1,4,256,768]{3,2,1,0:T(8,128)(2,1)S(1)}, bf16[1,4,256,768]{3,2,1,0:T(8,128)(2,1)}, u32[]{:S(2)}) copy-start(bf16[1,4,256,768]{3,2,1,0:T(8,128)(2,1)} %get-tuple-element.28.dx_in) | copy-start | bytes 4718596
